TPU v7x, 32 devices: a whole 2x2x4 slice. The times are simulated.
32 devices in a mesh: groups: 2 (over y), cache: 4 (over z), mp: 2 (over x), sub: 2 (over core).
Axes of the slice: x: 2, y: 2, z: 4, core: 2. Of those that a mesh axis runs over, the one named last changes fastest.
Arguments:
- conv_input: bfloat16 [8, 256, 20480], P(('groups', 'cache'), None, ('mp', 'sub')), parts along dimension 0, may hold values from -6 to 6
- dt_raw: float32 [8, 256, 256], P(('groups', 'cache'), None, ('mp', 'sub')), parts along dimension 0
- conv_weight: float32 [4, 20480], P(None, ('mp', 'sub')), may hold values from -3 to 3
- conv_bias: float32 [20480], P(('mp', 'sub')), may hold values from -3 to 3
- dt_bias: float32 [256], P(('mp', 'sub')), may hold values from -4.5 to -1.5
- a_log: float32 [256], P(('mp', 'sub')), may hold values from -4.5 to 0.5
- d_skip: float32 [256], P(('mp', 'sub')), may hold values from 0.5 to 1.5
- cache_state: bfloat16 [8, 256, 64, 256], P(('groups', 'cache'), ('mp', 'sub')), parts along dimension 0, may hold values from -2 to 2
- cache_tail: bfloat16 [8, 3, 20480], P(('groups', 'cache'), None, ('mp', 'sub')), parts along dimension 0, may hold values from -6 to 6
- hit_slot: int32 [8], P(('groups', 'cache')), parts along dimension 0, may hold values from 0 to 3, as said below
- hit_mask: int32 [8], P(('groups', 'cache')), parts along dimension 0, may hold values 0 or 1
- suffix_len: int32 [8], P(('groups', 'cache')), parts along dimension 0, may hold values from 32 to 256
- write_slot: int32 [8], P(('groups', 'cache')), parts along dimension 0, may hold values from 0 to 3, as said below
Outputs:
- y_out: bfloat16 [8, 256, 16384], P(('groups', 'cache'), None, ('mp', 'sub')), parts along dimension 0
- new_state: bfloat16 [8, 256, 64, 256], P(('groups', 'cache'), ('mp', 'sub')), parts along dimension 0
- new_tail: bfloat16 [8, 3, 20480], P(('groups', 'cache'), None, ('mp', 'sub')), parts along dimension 0
There are 2 independent parts, one for each index of `groups`. A program takes and returns all parts, laid end to end along the dimension named above; an argument that names none is the same for every part. Nothing has to cross between parts.
Inputs may be any that keep to these rules, and one draw needn't show every extreme that they name: `hit_slot`: owner of slot s is index s // 1 of cache; about half of the requests share one drawn slot. `write_slot`: each slot once; slot w belongs to index w // 1 of cache.
All inputs are finite; a program needn't handle non-finite values. No bound on the sum of `hit_mask` on one device may be relied on, other than what follows from the above.
Results may differ from a plain program's by a relative error of at most 0.001.
Values may be sent and summed in bfloat16 or wider, within the bound.
A program may use at most 128 MiB of HBM per device.

v0:
```python
import jax
import jax.numpy as jnp
from jax import lax
from jax.sharding import PartitionSpec as P

HEADS = 256
HEAD_P = 64
NSTATE = 256
GROUPS = 8
SPAN = 256


highest = lax.Precision.HIGHEST


def conv_and_scan(
    conv_input,
    dt_raw,
    prev_state,
    prev_tail,
    length,
    conv_weight,
    conv_bias,
    dt_bias,
    a_log,
    d_skip,
):
    steps_total = conv_input.shape[0]
    conv_width = conv_weight.shape[0]
    head_count = dt_raw.shape[1]
    per_group = HEADS // GROUPS
    groups_here = head_count // per_group
    x_width = per_group * HEAD_P
    extended = jnp.concatenate([prev_tail, conv_input.astype(jnp.float32)], axis=0)
    conv_sum = conv_bias[None, :] + conv_weight[0][None, :] * extended[0:steps_total]
    for shift_k in range(1, conv_width):
        conv_sum = (
            conv_sum + conv_weight[shift_k][None, :] * extended[shift_k : shift_k + steps_total]
        )
    activated = jax.nn.silu(conv_sum).reshape(steps_total, groups_here, x_width + 2 * NSTATE)
    x_heads = activated[:, :, :x_width].reshape(steps_total, groups_here, per_group, HEAD_P)
    b_group = activated[:, :, x_width : x_width + NSTATE]
    output_coeff_group = activated[:, :, x_width + NSTATE :]
    tail_rows = lax.dynamic_slice_in_dim(extended, length, conv_width - 1, 0)
    position = jnp.arange(steps_total, dtype=jnp.int32)
    live_mask = (position < length).astype(jnp.float32)
    step_size = jax.nn.softplus(dt_raw + dt_bias[None, :]) * live_mask[:, None]
    log_decay = (step_size * (-jnp.exp(a_log))[None, :]).reshape(
        steps_total, groups_here, per_group
    )
    x_scaled = x_heads * step_size.reshape(steps_total, groups_here, per_group)[..., None]
    carry_state = prev_state.reshape(groups_here, per_group, HEAD_P, NSTATE)
    tri_mask = jnp.tril(jnp.ones((SPAN, SPAN), dtype=bool))
    cum_decay = jnp.cumsum(log_decay, axis=0)
    gap_grid = jnp.where(
        tri_mask[:, :, None, None], cum_decay[:, None] - cum_decay[None, :], -jnp.inf
    )
    decay_grid = jnp.exp(gap_grid)
    intersection = jnp.einsum("ign,jgn->ijg", output_coeff_group, b_group, precision=highest)
    weighted = decay_grid * intersection[..., None]
    inner_part = jnp.einsum("ijgk,jgkp->igkp", weighted, x_scaled, precision=highest)
    carried_over = (
        jnp.einsum("ign,gkpn->igkp", output_coeff_group, carry_state, precision=highest)
        * jnp.exp(cum_decay)[..., None]
    )
    tail_decay = jnp.exp(cum_decay[-1][None] - cum_decay)
    x_tail = x_scaled * tail_decay[..., None]
    state_add = jnp.einsum("jgkp,jgn->gkpn", x_tail, b_group, precision=highest)
    carry_state = jnp.exp(cum_decay[-1])[..., None, None] * carry_state + state_add
    pieces_out = [inner_part + carried_over]
    y_heads = (
        jnp.concatenate(pieces_out, axis=0)
        + d_skip.reshape(groups_here, per_group)[None, :, :, None] * x_heads
    )
    y_heads = y_heads * live_mask[:, None, None, None]
    return (
        y_heads.reshape(steps_total, head_count * HEAD_P),
        carry_state.reshape(head_count, HEAD_P, NSTATE),
        tail_rows,
        output_coeff_group,
        log_decay,
        live_mask,
    )


def per_device(
    conv_input,
    dt_raw,
    conv_weight,
    conv_bias,
    dt_bias,
    a_log,
    d_skip,
    cache_state,
    cache_tail,
    hit_slot,
    hit_mask,
    suffix_len,
    write_slot,
):
    req_here = conv_input.shape[0]
    steps_total = conv_input.shape[1]
    slots_here = cache_state.shape[0]
    head_count = cache_state.shape[1]
    channels = cache_tail.shape[2]
    tail_count = cache_tail.shape[1]
    per_group = HEADS // GROUPS
    groups_here = head_count // per_group
    owners = lax.axis_size("cache")
    request_total = req_here * owners
    state_flat = cache_state.reshape(slots_here, head_count * HEAD_P * NSTATE)
    tail_flat = cache_tail.reshape(slots_here, tail_count * channels)
    all_slot, all_mask, all_write = (
        lax.all_gather(hit_slot, "cache", axis=0, tiled=True),
        lax.all_gather(hit_mask, "cache", axis=0, tiled=True),
        lax.all_gather(write_slot, "cache", axis=0, tiled=True),
    )
    hit_rows = all_mask[:, None] > 0

    def one_request(request_items):
        return conv_and_scan(
            request_items[0],
            request_items[1],
            request_items[2],
            request_items[3],
            request_items[4],
            conv_weight,
            conv_bias,
            dt_bias,
            a_log,
            d_skip,
        )

    tails_whole = lax.all_gather(tail_flat, "cache", axis=0, tiled=True)
    own_hits = hit_mask[:, None] > 0
    picked_tail = jnp.where(own_hits, tails_whole[hit_slot], jnp.zeros((), jnp.bfloat16))
    prev_tail = picked_tail.reshape(req_here, tail_count, channels).astype(jnp.float32)
    zero_state = jnp.zeros((req_here, head_count, HEAD_P, NSTATE), jnp.float32)
    results = lax.map(one_request, (conv_input, dt_raw, zero_state, prev_tail, suffix_len))
    y_local, final_states, tail_local, c_rows, log_decays, live_rows = results
    state_parts = lax.all_to_all(state_flat, "cache", split_axis=1, concat_axis=0, tiled=True)
    chosen_state = jnp.where(hit_rows, state_parts[all_slot], jnp.zeros((), jnp.bfloat16))
    fetched_state = lax.all_to_all(chosen_state, "cache", split_axis=0, concat_axis=1, tiled=True)
    start_state = fetched_state.reshape(req_here, head_count, HEAD_P, NSTATE).astype(jnp.float32)
    start_grouped = start_state.reshape(req_here, groups_here, per_group, HEAD_P, NSTATE)
    full_decay = jnp.cumsum(log_decays, axis=1)
    prefix_term = jnp.einsum("rign,rgkpn->rigkp", c_rows, start_grouped, precision=highest)
    prefix_term = prefix_term * jnp.exp(full_decay)[..., None] * live_rows[:, :, None, None, None]
    y_local = y_local + prefix_term.reshape(req_here, steps_total, head_count * HEAD_P)
    end_decay = jnp.exp(full_decay[:, -1]).reshape(req_here, head_count)
    final_states = final_states + end_decay[:, :, None, None] * start_state
    send_state = final_states.astype(jnp.bfloat16).reshape(req_here, head_count * HEAD_P * NSTATE)
    send_tail = tail_local.astype(jnp.bfloat16).reshape(req_here, tail_count * channels)
    spread_state, spread_tail = (
        lax.all_to_all(send_state, "cache", split_axis=1, concat_axis=0, tiled=True),
        lax.all_to_all(send_tail, "cache", split_axis=1, concat_axis=0, tiled=True),
    )
    request_ids = jnp.arange(request_total, dtype=jnp.int32)
    match_grid = all_write[None, :] == request_ids[:, None]
    inverse = jnp.sum(jnp.where(match_grid, request_ids[None, :], 0), axis=1)
    ordered_state = spread_state[inverse]
    ordered_tail = spread_tail[inverse]
    owned_state, owned_tail = (
        lax.all_to_all(ordered_state, "cache", split_axis=0, concat_axis=1, tiled=True),
        lax.all_to_all(ordered_tail, "cache", split_axis=0, concat_axis=1, tiled=True),
    )
    return (
        y_local.astype(jnp.bfloat16),
        owned_state.reshape(req_here, head_count, HEAD_P, NSTATE),
        owned_tail.reshape(req_here, tail_count, channels),
    )


def solution(mesh):
    placed = (
        P(("groups", "cache"), None, ("mp", "sub")),
        P(("groups", "cache"), None, ("mp", "sub")),
        P(None, ("mp", "sub")),
        P(("mp", "sub")),
        P(("mp", "sub")),
        P(("mp", "sub")),
        P(("mp", "sub")),
        P(("groups", "cache"), ("mp", "sub"), None, None),
        P(("groups", "cache"), None, ("mp", "sub")),
        P(("groups", "cache")),
        P(("groups", "cache")),
        P(("groups", "cache")),
        P(("groups", "cache")),
    )
    return jax.shard_map(
        per_device,
        mesh=mesh,
        in_specs=placed,
        out_specs=(
            P(("groups", "cache"), None, ("mp", "sub")),
            P(("groups", "cache"), ("mp", "sub"), None, None),
            P(("groups", "cache"), None, ("mp", "sub")),
        ),
        check_vma=False,
    )
```

profile of v0, /device:TPU:0, one launch (start us, length us, event | category | flops | bytes accessed | tf_op | source)
XLA Modules:
  0.0 417.7 jit_solution(16743109034872227614)
XLA Ops:
  5.7 14.2 %reduce.9 = bf16[4,262144]{1,0:T(4,128)(2,1)S(1)} reduce(bf16[4,1,262144]{2,1,0:T(2,128)(2,1)} %bitcast.136, bf16[]{:T(256)} %broadcast.245), dimensions={1}, to_apply=%bitcast.107.reduce_sub_computation | reduce | bytes 4194306
  23.4 6.3 %all-to-all-start = ((bf16[4,2,131072]{2,1,0:T(2,128)(2,1)}), bf16[4,2,131072]{2,1,0:T(2,128)(2,1)S(1)}, u32[]{:S(2)}, u32[]{:S(2)}) async-start(bf16[4,2,131072]{2,1,0:T(2,128)(2,1)} %reshape.568), calls=%async_computation | async-start | bytes 4194304 | tf_op jit(solution)/shard_map/all_to_all | solution.py:141
  38.4 47.0 %all-gather = bf16[4,1,15360]{2,1,0:T(2,128)(2,1)S(1)} all-gather(bf16[1,1,15360]{2,1,0:T(2,128)(2,1)S(1)} %reshape.537), channel_id=1, replica_groups=mesh['groups'=2,'cache'=4,'mp'=2,'sub'=2] {'cache'}, dimensions={0}, use_global_device_ids=true | all-gather | bytes 153600 | tf_op jit(solution)/shard_map/all_gather | solution.py:134
  88.1 8.2 %all-reduce.3 = (s32[4]{0:T(128)S(1)}, s32[4]{0:T(128)S(1)}, s32[4]{0:T(128)}) all-reduce(s32[4]{0:T(128)S(1)} %dynamic-update-slice.2, s32[4]{0:T(128)S(1)} %dynamic-update-slice.1, s32[4]{0:T(128)S(1)} %dynamic-update-slice.3), channel_id=1, replica_groups=mesh['groups'=2,'cache'=4,'mp'=2,'sub'=2] {'cache'}, use_global_device_ids=true, to_apply=%add.1 | all-reduce | flops 12 | bytes 96
  98.7 7.2 %mul.283 = f32[1,4,262144]{2,0,1:T(1,128)} reshape(f32[64,64,256]{2,1,0:T(8,128)} %mul.282) | data formatting | bytes 8388608 | tf_op jit(solution)/shard_map/mul | solution.py:151
  107.1 4.7 %bitcast_convert_fusion = f32[256,5120]{1,0:T(8,128)} fusion(bf16[1,256,5120]{2,1,0:T(8,128)(2,1)} %param.13), kind=kLoop, calls=%fused_computation.47 | loop fusion | flops 1310720 | bytes 7864320 | tf_op jit(solution)/shard_map/while/body/eval_jaxpr/convert_element_type | solution.py:34
  115.1 5.9 %copy.188 = bf16[1,4,262144]{2,1,0:T(4,128)(2,1)S(1)} copy(bf16[1,4,262144]{2,0,1:T(2,128)(2,1)} %bitcast.137) | data formatting | bytes 4194304
  126.4 12.3 %fusion.37 = bf16[4,1,262144]{2,0,1:T(4,128)(2,1)S(1)} fusion(bf16[4,87296]{1,0:T(4,128)(2,1)} %gather_fusion.3, bf16[4,87424]{1,0:T(4,128)(2,1)S(1)} %gather_fusion.2, bf16[4,87424]{1,0:T(4,128)(2,1)S(1)} %gather_fusion.1, pred[4]{0:T(512)(128)(4,1)S(1)} %copy-done.17), kind=kLoop, calls=%fused_computation.50 | loop fusion | flops 7340032 | bytes 4194308 | tf_op jit(solution)/shard_map/jit(_where)/select_n | solution.py:142
  138.7 4.6 %reduce.10 = bf16[4,262144]{1,0:T(4,128)(2,1)} reduce(bf16[4,1,262144]{2,0,1:T(4,128)(2,1)S(1)} %fusion.37, bf16[]{:T(256)} %broadcast.245), dimensions={1}, to_apply=%copy.155.reduce_sub_computation | reduce | bytes 4194306 | tf_op jit(solution)/shard_map/jit(_where)/select_n | solution.py:142
  143.4 5.0 %reshape.570 = bf16[4,2,131072]{2,1,0:T(2,128)(2,1)} reshape(bf16[4,262144]{1,0:T(4,128)(2,1)} %reduce.10) | data formatting | bytes 4194304
  152.3 10.8 %divide_multiply_fusion = f32[256,5120]{1,0:T(8,128)} fusion(f32[256,5120]{1,0:T(8,128)} %bitcast_convert_fusion, f32[3,5120]{1,0:T(4,128)S(1)} %copy-done.5, f32[5120]{0:T(1024)S(1)} %bitcast.156, f32[5120]{0:T(1024)S(1)} %bitcast.157, f32[5120]{0:T(1024)S(1)} %bitcast.155, f32[5120]{0:T(1024)S(1)} %bitcast.154, f32[5120]{0:T(1024)S(1)} %copy-done.16), kind=kLoop, calls=%fused_computation.31 | loop fusion | flops 19660800 | bytes 10649600 | tf_op jit(solution)/shard_map/while/body/eval_jaxpr/jit(silu)/mul | solution.py:40
  163.1 5.9 %copy.146 = f32[256,5120]{0,1:T(8,128)} copy(f32[256,5120]{1,0:T(8,128)} %divide_multiply_fusion) | data formatting | bytes 10485760 | tf_op jit(solution)/shard_map/while/body/eval_jaxpr/jit(silu)/mul | solution.py:40
  176.2 6.5 %fusion.34 = f32[2,32,64,256]{3,2,1,0:T(8,128)} fusion(f32[256,2,32,64]{0,3,2,1:T(8,128)S(1)} %bitcast.133, f32[256,2,32]{0,2,1:T(8,128)S(1)} %get-tuple-element.77, f32[2,32]{1,0:T(2,128)S(1)} %exponential_multiply_fusion, f32[256,2,32]{0,2,1:T(8,128)S(1)} %copy-done.6, f32[256,2,2560]{0,2,1:T(8,128)} %bitcast.129), kind=kOutput, calls=%fused_computation.48 | convolution fusion | flops 3224371200 | bytes 9044224 | tf_op jit(solution)/shard_map/while/body/eval_jaxpr/jgkp,jgn->gkpn/dot_general | solution.py:68
  182.7 7.1 %broadcast_in_dim.136 = f32[1,4,262144]{2,0,1:T(1,128)} reshape(f32[2,32,64,256]{3,2,1,0:T(8,128)} %fusion.34) | data formatting | bytes 8388608 | tf_op jit(solution)/shard_map/while/body/jit(dynamic_update_index_in_dim)/broadcast_in_dim | solution.py:139
  189.8 5.9 %all-to-all-done.1 = bf16[4,2,131072]{2,1,0:T(2,128)(2,1)S(1)} async-done(((bf16[4,2,131072]{2,1,0:T(2,128)(2,1)}), bf16[4,2,131072]{2,1,0:T(2,128)(2,1)S(1)}, u32[]{:S(2)}, u32[]{:S(2)}) %all-to-all-start.1) | async-done | bytes 2097184 | tf_op jit(solution)/shard_map/all_to_all | solution.py:143
  202.4 9.6 %fusion.67 = bf16[4,1,262144]{2,1,0:T(2,128)(2,1)} fusion(f32[1,4,262144]{2,0,1:T(1,128)} %broadcast_in_dim.136, f32[1,4,262144]{2,0,1:T(1,128)} %mul.283, bf16[4,1,262144]{2,1,0:T(2,128)(2,1)} %reshape.571), kind=kLoop, calls=%fused_computation.108 | loop fusion | flops 4194304 | bytes 12582912
  211.9 14.2 %reduce.11 = bf16[4,262144]{1,0:T(4,128)(2,1)S(1)} reduce(bf16[4,1,262144]{2,1,0:T(2,128)(2,1)} %fusion.67, bf16[]{:T(256)} %broadcast.245), dimensions={1}, to_apply=%fusion.67.reduce_sub_computation | reduce | bytes 4194306
  229.6 5.0 %all-to-all-start.2 = ((bf16[4,2,131072]{2,1,0:T(2,128)(2,1)}), bf16[4,2,131072]{2,1,0:T(2,128)(2,1)S(1)}, u32[]{:S(2)}, u32[]{:S(2)}) async-start(bf16[4,2,131072]{2,1,0:T(2,128)(2,1)} %reshape.572), calls=%async_computation.2 | async-start | bytes 4194304 | tf_op jit(solution)/shard_map/all_to_all | solution.py:155
  236.7 45.0 %all-to-all-done.2 = bf16[4,2,131072]{2,1,0:T(2,128)(2,1)S(1)} async-done(((bf16[4,2,131072]{2,1,0:T(2,128)(2,1)}), bf16[4,2,131072]{2,1,0:T(2,128)(2,1)S(1)}, u32[]{:S(2)}, u32[]{:S(2)}) %all-to-all-start.2) | async-done | bytes 2097184 | tf_op jit(solution)/shard_map/all_to_all | solution.py:155
  288.9 5.9 %copy.187 = bf16[1,4,262144]{2,1,0:T(4,128)(2,1)S(1)} copy(bf16[1,4,262144]{2,0,1:T(2,128)(2,1)} %bitcast.138) | data formatting | bytes 4194304
  300.1 12.3 %maximum_bitcast_fusion.1 = bf16[4,1,262144]{2,0,1:T(4,128)(2,1)S(1)} fusion(bf16[4,87296]{1,0:T(4,128)(2,1)} %gather_fusion.6, bf16[4,87424]{1,0:T(4,128)(2,1)S(1)} %gather_fusion.5, bf16[4,87424]{1,0:T(4,128)(2,1)S(1)} %gather_fusion.4), kind=kLoop, calls=%fused_computation.51 | loop fusion | flops 6291456 | bytes 4194304 | tf_op jit(solution)/shard_map/all_to_all | solution.py:164
  312.4 4.6 %reduce.12 = bf16[4,262144]{1,0:T(4,128)(2,1)} reduce(bf16[4,1,262144]{2,0,1:T(4,128)(2,1)S(1)} %maximum_bitcast_fusion.1, bf16[]{:T(256)} %broadcast.245), dimensions={1}, to_apply=%copy.166.reduce_sub_computation | reduce | bytes 4194306 | tf_op jit(solution)/shard_map/all_to_all | solution.py:164
  317.1 5.1 %reshape.574 = bf16[4,2,131072]{2,1,0:T(2,128)(2,1)} reshape(bf16[4,262144]{1,0:T(4,128)(2,1)} %reduce.12) | data formatting | bytes 4194304
  322.2 5.1 %all-to-all-start.3 = ((bf16[4,2,131072]{2,1,0:T(2,128)(2,1)}), bf16[4,2,131072]{2,1,0:T(2,128)(2,1)S(1)}, u32[]{:S(2)}, u32[]{:S(2)}) async-start(bf16[4,2,131072]{2,1,0:T(2,128)(2,1)} %reshape.574), calls=%async_computation.3 | async-start | bytes 4194304 | tf_op jit(solution)/shard_map/all_to_all | solution.py:164
  334.7 19.8 %fusion.25 = f32[256,2,32,64]{0,3,2,1:T(8,128)} fusion(f32[2,32,64,256]{3,2,1,0:T(8,128)S(1)} %fusion.39, f32[256,2,32,64]{0,3,2,1:T(8,128)S(1)} %bitcast.134, f32[256,256,2]{1,0,2:T(8,128)S(1)} %copy.153, f32[256,2,32]{0,2,1:T(8,128)S(1)} %copy-done.10, pred[256,256]{1,0:T(8,128)(4,1)S(1)} %iota_compare_fusion, f32[256]{0:T(256)S(1)} %compare_convert_fusion, ...), kind=kOutput, calls=%fused_computation.41 | convolution fusion | flops 3240099840 | bytes 13370624 | tf_op jit(solution)/shard_map/while/body/eval_jaxpr/ijgk,jgkp->igkp/dot_general | solution.py:61
  354.4 5.7 %copy.163 = f32[1,256,4096]{2,1,0:T(8,128)} copy(f32[1,256,4096]{1,2,0:T(8,128)} %bitcast.143) | data formatting | bytes 8388608 | tf_op jit(solution)/shard_map/while/body/jit(dynamic_update_index_in_dim)/broadcast_in_dim | solution.py:139
  360.9 15.0 %reduce.1 = bf16[4,262144]{1,0:T(4,128)(2,1)} reduce(bf16[4,1,262144]{2,1,0:T(2,128)(2,1)} %reshape.571, bf16[]{:T(256)} %constant.118), dimensions={1}, to_apply=%all_to_all.65.reduce_sub_computation | reduce | bytes 4194306 | tf_op jit(solution)/shard_map/all_to_all | solution.py:143
  376.0 4.8 %reshape.436 = bf16[2,32,64,256]{3,2,1,0:T(8,128)(2,1)} reshape(bf16[4,262144]{1,0:T(4,128)(2,1)} %reduce.1) | data formatting | bytes 4194304 | tf_op jit(solution)/shard_map/reshape.43
  380.8 5.7 %fusion.22 = f32[1,256,2,32,64]{1,4,3,2,0:T(8,128)} fusion(bf16[2,32,64,256]{3,2,1,0:T(8,128)(2,1)} %reshape.436, f32[256]{0:T(256)S(1)} %compare_convert_fusion, f32[256,2,32]{0,2,1:T(8,128)S(1)} %copy.162, f32[256,2,2560]{0,2,1:T(8,128)} %bitcast.132), kind=kOutput, calls=%fused_computation.37 | convolution fusion | flops 3223322624 | bytes 6882304 | tf_op jit(solution)/shard_map/rign,rgkpn->rigkp/dot_general | solution.py:147
  386.5 5.6 %copy.164 = f32[1,256,4096]{2,1,0:T(8,128)} copy(f32[1,256,4096]{1,2,0:T(8,128)} %bitcast.135) | data formatting | bytes 8388608 | tf_op jit(solution)/shard_map/reshape | solution.py:149
  392.1 5.3 %add_convert_fusion = bf16[1,256,4096]{2,1,0:T(8,128)(2,1)} fusion(f32[1,256,4096]{2,1,0:T(8,128)} %copy.163, f32[1,256,4096]{2,1,0:T(8,128)} %copy.164), kind=kLoop, calls=%fused_computation.44 | loop fusion | flops 2097152 | bytes 10485760 | tf_op jit(solution)/shard_map/convert_element_type | solution.py:168
  400.7 13.5 %reduce.3 = bf16[4,262144]{1,0:T(4,128)(2,1)S(1)} reduce(bf16[4,1,262144]{2,1,0:T(2,128)(2,1)} %reshape.575, bf16[]{:T(256)} %constant.118), dimensions={1}, to_apply=%all_to_all.69.reduce_sub_computation | reduce | bytes 4194306 | tf_op jit(solution)/shard_map/all_to_all | solution.py:164
  (139 shorter events, 79.6 us)
Async XLA Ops:
  19.9 10.5 %copy-start.18 = (f32[64]{0:T(128)S(1)}, f32[64]{0:T(128)}, u32[]{:S(2)}) copy-start(f32[64]{0:T(128)} %param.18) | copy-start | bytes 772
  19.9 10.6 %copy-start.19 = (f32[64]{0:T(128)S(1)}, f32[64]{0:T(128)}, u32[]{:S(2)}) copy-start(f32[64]{0:T(128)} %param.17) | copy-start | bytes 772
  19.9 10.6 %copy-start.8 = (f32[1,256,64]{1,2,0:T(8,128)S(1)}, f32[1,256,64]{1,2,0:T(8,128)}, u32[]{:S(2)}) copy-start(f32[1,256,64]{1,2,0:T(8,128)} %param.14) | copy-start | bytes 196612
  19.9 14.1 %copy-start.22 = (u32[32]{0:T(128)S(1)}, u32[32]{0:T(128)}, u32[]{:S(2)}) copy-start(u32[32]{0:T(128)} %constant.100) | copy-start | bytes 388
  19.9 16.2 %copy-start.15 = (bf16[1,3,5120]{2,1,0:T(4,128)(2,1)S(1)}, bf16[1,3,5120]{2,1,0:T(4,128)(2,1)}, u32[]{:S(2)}) copy-start(bf16[1,3,5120]{2,1,0:T(4,128)(2,1)} %param.21) | copy-start | bytes 92164
  23.4 88.5 %all-to-all-start = ((bf16[4,2,131072]{2,1,0:T(2,128)(2,1)}), bf16[4,2,131072]{2,1,0:T(2,128)(2,1)S(1)}, u32[]{:S(2)}, u32[]{:S(2)}) async-start(bf16[4,2,131072]{2,1,0:T(2,128)(2,1)} %reshape.568), calls=%async_computation | async-start | bytes 4194304 | tf_op jit(solution)/shard_map/all_to_all | solution.py:141
  38.2 48.1 %copy-start.3 = (f32[32,2,2,128]{3,0,1,2:T(8,128)}, f32[32,2,2,128]{3,0,1,2:T(8,128)S(1)}, u32[]{:S(2)}) copy-start(f32[32,2,2,128]{3,0,1,2:T(8,128)S(1)} %reduce-window.14) | copy-start | bytes 196612
  98.7 7.8 %copy-start.13 = (f32[4,5120]{1,0:T(4,128)S(1)}, f32[4,5120]{1,0:T(4,128)}, u32[]{:S(2)}) copy-start(f32[4,5120]{1,0:T(4,128)} %param.15) | copy-start | bytes 245764
  125.1 1.2 copy-start.17
  143.4 8.9 %copy-start.5 = (f32[3,5120]{1,0:T(4,128)S(1)}, f32[3,5120]{1,0:T(4,128)}, u32[]{:S(2)}) copy-start(f32[3,5120]{1,0:T(4,128)} %reshape.465) | copy-start | bytes 184324
  143.4 8.9 %copy-start.11 = (f32[1,5120]{1,0:T(1,128)S(1)}, f32[1,5120]{1,0:T(1,128)}, u32[]{:S(2)}) copy-start(f32[1,5120]{1,0:T(1,128)} %get-tuple-element.75) | copy-start | bytes 61444
  143.4 8.9 %copy-start.12 = (f32[1,5120]{1,0:T(1,128)S(1)}, f32[1,5120]{1,0:T(1,128)}, u32[]{:S(2)}) copy-start(f32[1,5120]{1,0:T(1,128)} %get-tuple-element.76) | copy-start | bytes 61444
  143.4 8.9 %copy-start.16 = (f32[5120]{0:T(1024)S(1)}, f32[5120]{0:T(1024)}, u32[]{:S(2)}) copy-start(f32[5120]{0:T(1024)} %param.16) | copy-start | bytes 61444
  148.4 47.4 %all-to-all-start.1 = ((bf16[4,2,131072]{2,1,0:T(2,128)(2,1)}), bf16[4,2,131072]{2,1,0:T(2,128)(2,1)S(1)}, u32[]{:S(2)}, u32[]{:S(2)}) async-start(bf16[4,2,131072]{2,1,0:T(2,128)(2,1)} %reshape.570), calls=%async_computation.1 | async-start | bytes 4194304 | tf_op jit(solution)/shard_map/all_to_all | solution.py:143
  171.6 2.5 copy-start.4
  171.6 4.7 %copy-start.6 = (f32[256,2,32]{0,2,1:T(8,128)S(1)}, f32[256,2,32]{0,2,1:T(8,128)}, u32[]{:S(2)}) copy-start(f32[256,2,32]{0,2,1:T(8,128)} %get-tuple-element.68) | copy-start | bytes 196612
  174.1 2.2 copy-start
  174.2 1.2 copy-start.9
  195.8 33.8 %all-to-all-start.4 = ((bf16[4,2,1920]{2,1,0:T(2,128)(2,1)}), bf16[4,2,1920]{2,1,0:T(2,128)(2,1)S(1)}, u32[]{:S(2)}, u32[]{:S(2)}) async-start(bf16[4,2,1920]{2,1,0:T(2,128)(2,1)} %reshape.576), calls=%async_computation.4 | async-start | bytes 61440 | tf_op jit(solution)/shard_map/all_to_all | solution.py:156
  226.1 8.5 %copy-start.21 = (s32[4]{0:T(128)S(1)}, s32[4]{0:T(128)}, u32[]{:S(2)}) copy-start(s32[4]{0:T(128)} %get-tuple-element.64) | copy-start | bytes 52
  229.6 52.2 %all-to-all-start.2 = ((bf16[4,2,131072]{2,1,0:T(2,128)(2,1)}), bf16[4,2,131072]{2,1,0:T(2,128)(2,1)S(1)}, u32[]{:S(2)}, u32[]{:S(2)}) async-start(bf16[4,2,131072]{2,1,0:T(2,128)(2,1)} %reshape.572), calls=%async_computation.2 | async-start | bytes 4194304 | tf_op jit(solution)/shard_map/all_to_all | solution.py:155
  281.7 40.4 %all-to-all-start.5 = ((bf16[4,2,1920]{2,1,0:T(2,128)(2,1)}), bf16[4,2,1920]{2,1,0:T(2,128)(2,1)S(1)}, u32[]{:S(2)}, u32[]{:S(2)}) async-start(bf16[4,2,1920]{2,1,0:T(2,128)(2,1)} %reshape.578), calls=%async_computation.5 | async-start | bytes 61440 | tf_op jit(solution)/shard_map/all_to_all | solution.py:165
  317.1 12.5 %copy-start.20 = (f32[64]{0:T(128)S(1)}, f32[64]{0:T(128)}, u32[]{:S(2)}) copy-start(f32[64]{0:T(128)} %param.19) | copy-start | bytes 772
  317.1 12.6 %copy-start.2 = (f32[256,2,32]{2,1,0:T(2,128)S(1)}, f32[256,2,32]{2,1,0:T(2,128)}, u32[]{:S(2)}) copy-start(f32[256,2,32]{2,1,0:T(2,128)} %get-tuple-element.65) | copy-start | bytes 196612
  322.2 75.2 %all-to-all-start.3 = ((bf16[4,2,131072]{2,1,0:T(2,128)(2,1)}), bf16[4,2,131072]{2,1,0:T(2,128)(2,1)S(1)}, u32[]{:S(2)}, u32[]{:S(2)}) async-start(bf16[4,2,131072]{2,1,0:T(2,128)(2,1)} %reshape.574), calls=%async_computation.3 | async-start | bytes 4194304 | tf_op jit(solution)/shard_map/all_to_all | solution.py:164
  327.2 7.4 %copy-start.7 = (f32[256,2,32]{0,2,1:T(8,128)S(1)}, f32[256,2,32]{0,2,1:T(8,128)}, u32[]{:S(2)}) copy-start(f32[256,2,32]{0,2,1:T(8,128)} %get-tuple-element.68) | copy-start | bytes 196612
  327.2 7.4 %copy-start.10 = (f32[256,2,32]{0,2,1:T(8,128)S(1)}, f32[256,2,32]{0,2,1:T(8,128)}, u32[]{:S(2)}) copy-start(f32[256,2,32]{0,2,1:T(8,128)} %copy-done.9) | copy-start | bytes 196612
  327.2 7.4 %copy-start.14 = (f32[256,2,32]{0,2,1:T(8,128)S(1)}, f32[256,2,32]{0,2,1:T(8,128)}, u32[]{:S(2)}) copy-start(f32[256,2,32]{0,2,1:T(8,128)} %get-tuple-element.78) | copy-start | bytes 196612
  329.9 4.7 %copy-start.1 = (f32[256,2,2048]{0,2,1:T(8,128)S(1)}, f32[256,2,2048]{0,2,1:T(8,128)}, u32[]{:S(2)}) copy-start(f32[256,2,2048]{0,2,1:T(8,128)} %copy-done) | copy-start | bytes 12582916
where the time goes:
time: 425 us; the launch traced here: 418 us
  other arithmetic  130 us (31%)
  local copies, waits for them, and re-layouts  111 us (26%)
  blocking collectives  55.2 us (13%)
  waiting for transfers between devices  50.9 us (12%)
  matrix products  38.8 us (9%)
  starting transfers between devices  27.2 us (6%)
    unnamed x70, local copies, waits for them, and re-layouts  48 us
    all_gather x1, blocking collectives, per_device(): tails_whole = lax.all_gather(tail_flat, 'cache', axis=0, tiled=True)  47 us
    all_to_all x1, waiting for transfers between devices, per_device(): lax.all_to_all(send_state, 'cache', split_axis=1, concat_axis=0, tiled=True)  45 us
    unnamed x5, other arithmetic  39.5 us
    all_to_all x3, other arithmetic, per_device(): lax.all_to_all(ordered_state, 'cache', split_axis=0, concat_axis=1, tiled...  30.4 us
    dot_general x1, matrix products, conv_and_scan(): jnp.einsum('ijgk,jgkp->igkp', weighted, x_scaled, precision=highest)  19.8 us
    select_n x2, other arithmetic, per_device(): jnp.where(hit_rows, state_parts[all_slot], jnp.zeros((), jnp.bfloat16))  17 us
    all_to_all x1, other arithmetic, per_device(): lax.all_to_all(chosen_state, 'cache', split_axis=0, concat_axis=1, tiled=...  15 us
  transfers between devices with their start and end apart: 6, of which 2 were waited for; matrix products, arithmetic and copies ran while one was open for 48% of the time, Pallas kernels for 0%

commit v1 on v0

v1 whole, which is shorter than its diff:
```python
import jax
import jax.numpy as jnp
from jax import lax
from jax.experimental import pallas as pl
from jax.experimental.pallas import tpu as pltpu
from jax.sharding import PartitionSpec as P

HEADS = 256
HEAD_P = 64
NSTATE = 256
GROUPS = 8
PER_GROUP = HEADS // GROUPS
HB = 8
HBW = HB * HEAD_P
BLOCKS = PER_GROUP // HB
VMEM = 56 * 1024 * 1024

highest = lax.Precision.HIGHEST
f32 = jnp.float32


def dot(a, b, dims):
    return lax.dot_general(a, b, (dims, ((), ())), precision=highest, preferred_element_type=f32)


def conv_silu(scratch, x_ref, tail_ref, w_ref, b_ref):
    steps = x_ref.shape[0]
    scratch[0:8, :] = tail_ref[...]
    scratch[8 : 8 + steps, :] = x_ref[...].astype(f32)
    total = b_ref[...]
    for k in range(4):
        total = total + w_ref[k : k + 1, :] * scratch[5 + k : 5 + k + steps, :]
    return total / (1.0 + jnp.exp(-total))


def widen(cols):
    head = lax.broadcasted_iota(jnp.int32, (HB, HBW), 0)
    lane = lax.broadcasted_iota(jnp.int32, (HB, HBW), 1)
    spread = jnp.where(lane // HEAD_P == head, 1.0, 0.0).astype(f32)
    return dot(cols, spread, ((1,), (0,)))


def scan_kernel(
    x_ref, bc_ref, tailx_ref, tailbc_ref, wx_ref, wbc_ref, bx_ref, bbc_ref,
    step_ref, cum_ref, cumt_ref, skip_ref,
    y_ref, c_ref, add_ref,
    scratch, b_s, cb_s,
):
    steps = x_ref.shape[0]

    @pl.when(pl.program_id(1) == 0)
    def _():
        bc = conv_silu(scratch, bc_ref, tailbc_ref, wbc_ref, bbc_ref)
        b_s[...] = bc[:, :NSTATE]
        c_ref[...] = bc[:, NSTATE:]
        cb = dot(bc[:, NSTATE:], bc[:, :NSTATE], ((1,), (1,)))
        row = lax.broadcasted_iota(jnp.int32, (steps, steps), 0)
        col = lax.broadcasted_iota(jnp.int32, (steps, steps), 1)
        cb_s[...] = jnp.where(row >= col, cb, 0.0)

    x = conv_silu(scratch, x_ref, tailx_ref, wx_ref, bx_ref)
    cum = cum_ref[0]
    x_scaled = x * widen(step_ref[0])
    x_tail = x_scaled * widen(jnp.exp(cum[steps - 1 : steps, :] - cum))
    add = dot(x_tail, b_s[...], ((0,), (0,)))
    add_ref[...] = add.reshape(HB, HEAD_P, NSTATE)
    lane = lax.broadcasted_iota(jnp.int32, (steps, 2 * HEAD_P), 1)
    for pair in range(HB // 2):
        lo, hi = pair * 2 * HEAD_P, (pair + 1) * 2 * HEAD_P
        both = x_scaled[:, lo:hi]
        parts = []
        for k in (2 * pair, 2 * pair + 1):
            gap = jnp.minimum(cum[:, k : k + 1] - cumt_ref[k : k + 1, :], 0.0)
            parts.append(dot(jnp.exp(gap) * cb_s[...], both, ((1,), (0,))))
        inner = jnp.where(lane < HEAD_P, parts[0], parts[1])
        y_ref[:, lo:hi] = inner + skip_ref[:, lo:hi] * x[:, lo:hi]


def prefix_kernel(len_ref, y_ref, c_ref, cum_ref, state_ref, out_ref):
    steps = y_ref.shape[0]
    state = state_ref[...].reshape(HBW, NSTATE).astype(f32)
    carried = dot(c_ref[...], state, ((1,), (1,)))
    total = y_ref[...] + carried * widen(jnp.exp(cum_ref[0]))
    row = lax.broadcasted_iota(jnp.int32, (steps, HBW), 0)
    out_ref[...] = jnp.where(row < len_ref[0], total, 0.0).astype(jnp.bfloat16)


def final_kernel(decay_ref, add_ref, state_ref, out_ref):
    base = pl.program_id(0) * HB
    for k in range(HB):
        out_ref[k] = (
            decay_ref[base + k] * state_ref[k].astype(f32) + add_ref[k]
        ).astype(jnp.bfloat16)


def choose_kernel(slot_ref, mask_ref, in_ref, out_ref):
    keep = mask_ref[pl.program_id(0)] > 0
    out_ref[...] = jnp.where(keep, in_ref[...], jnp.zeros_like(in_ref))


def choose(parts, slot, mask):
    count = parts.shape[0]
    block = (1,) + parts.shape[1:]
    return pl.pallas_call(
        choose_kernel,
        grid_spec=pltpu.PrefetchScalarGridSpec(
            num_scalar_prefetch=2,
            grid=(count,),
            in_specs=[pl.BlockSpec(block, lambda r, s, m: (s[r], 0, 0, 0))],
            out_specs=pl.BlockSpec(block, lambda r, s, m: (r, 0, 0, 0)),
        ),
        out_shape=jax.ShapeDtypeStruct(parts.shape, parts.dtype),
        compiler_params=pltpu.CompilerParams(vmem_limit_bytes=VMEM),
        cost_estimate=pl.CostEstimate(flops=0, bytes_accessed=4 * parts.size, transcendentals=0),
    )(slot, mask, parts)


def move_state(state, slot, mask):
    n = lax.axis_size("cache")
    pieces = state.reshape(n, state.shape[0] // n, HEAD_P, NSTATE)
    parts = lax.all_to_all(pieces, "cache", split_axis=0, concat_axis=0, tiled=True)
    chosen = choose(parts, slot, mask)
    return lax.all_to_all(chosen, "cache", split_axis=0, concat_axis=0, tiled=True).reshape(
        state.shape
    )


def per_device(
    conv_input, dt_raw, conv_weight, conv_bias, dt_bias, a_log, d_skip,
    cache_state, cache_tail, hit_slot, hit_mask, suffix_len, write_slot,
):
    conv = conv_input[0]
    steps, channels = conv.shape
    heads = dt_raw.shape[2]
    tail_count = cache_tail.shape[1]
    groups_here = heads // PER_GROUP
    blocks = groups_here * BLOCKS
    n = lax.axis_size("cache")
    me = lax.axis_index("cache")

    new_tail = lax.dynamic_slice_in_dim(conv, suffix_len[0] - tail_count, tail_count, 0)
    ints = jnp.concatenate([hit_slot, hit_mask, write_slot]).astype(jnp.bfloat16)
    row = jnp.concatenate(
        [
            cache_tail.reshape(-1, 128),
            new_tail.reshape(-1, 128),
            jnp.pad(ints, (0, 125)).reshape(1, 128),
        ],
        axis=0,
    )
    rows = lax.all_to_all(
        jnp.broadcast_to(row[None], (n,) + row.shape), "cache", split_axis=0, concat_axis=0,
        tiled=True,
    )
    table = rows[:, -1, :3].astype(jnp.int32)
    all_slot, all_mask, all_write = table[:, 0], table[:, 1], table[:, 2]
    ids = jnp.arange(n, dtype=jnp.int32)
    inverse = jnp.sum(jnp.where(all_write[None, :] == ids[:, None], ids[None, :], 0), axis=1)
    tail_rows = tail_count * channels // 128
    start_tail = lax.dynamic_index_in_dim(rows[:, :tail_rows], hit_slot[0], 0, keepdims=False)
    start_tail = jnp.where(hit_mask[0] > 0, start_tail, jnp.zeros((), jnp.bfloat16))
    start_tail = start_tail.reshape(tail_count, channels).astype(f32)
    tail8 = jnp.pad(start_tail, ((8 - tail_count, 0), (0, 0)))
    out_tail = lax.dynamic_index_in_dim(
        rows[:, tail_rows : 2 * tail_rows], inverse[me], 0, keepdims=False
    ).reshape(1, tail_count, channels)

    position = lax.broadcasted_iota(jnp.int32, (steps, 1), 0)
    step = jax.nn.softplus(dt_raw[0] + dt_bias[None, :]) * (position < suffix_len[0]).astype(f32)
    cum = jnp.cumsum(step * (-jnp.exp(a_log))[None, :], axis=0)
    step_b = step.reshape(steps, blocks, HB).transpose(1, 0, 2)
    cum_b = cum.reshape(steps, blocks, HB).transpose(1, 0, 2)
    end_decay = jnp.exp(cum[-1])
    skip_wide = jnp.repeat(d_skip, HEAD_P).reshape(1, heads * HEAD_P)
    bias = conv_bias.reshape(1, channels)

    wide = BLOCKS + 1

    def xs(rows_):
        return pl.BlockSpec((rows_, HBW), lambda g, b: (0, g * wide + b))

    def bcs(rows_):
        return pl.BlockSpec((rows_, HBW), lambda g, b: (0, g * wide + BLOCKS))

    per_block = pl.BlockSpec((1, steps, HB), lambda g, b: (g * BLOCKS + b, 0, 0))
    y_part, c_rows, add = pl.pallas_call(
        scan_kernel,
        grid=(groups_here, BLOCKS),
        in_specs=[
            xs(steps), bcs(steps), xs(8), bcs(8), xs(4), bcs(4), xs(1), bcs(1),
            per_block, per_block,
            pl.BlockSpec((HB, steps), lambda g, b: (g * BLOCKS + b, 0)),
            pl.BlockSpec((1, HBW), lambda g, b: (0, g * BLOCKS + b)),
        ],
        out_specs=[
            pl.BlockSpec((steps, HBW), lambda g, b: (0, g * BLOCKS + b)),
            pl.BlockSpec((steps, NSTATE), lambda g, b: (0, g)),
            pl.BlockSpec((HB, HEAD_P, NSTATE), lambda g, b: (g * BLOCKS + b, 0, 0)),
        ],
        out_shape=[
            jax.ShapeDtypeStruct((steps, heads * HEAD_P), f32),
            jax.ShapeDtypeStruct((steps, groups_here * NSTATE), f32),
            jax.ShapeDtypeStruct((heads, HEAD_P, NSTATE), f32),
        ],
        scratch_shapes=[
            pltpu.VMEM((steps + 8, HBW), f32),
            pltpu.VMEM((steps, NSTATE), f32),
            pltpu.VMEM((steps, steps), f32),
        ],
        compiler_params=pltpu.CompilerParams(vmem_limit_bytes=VMEM),
        cost_estimate=pl.CostEstimate(
            flops=20_000_000_000, bytes_accessed=12_000_000, transcendentals=6_000_000
        ),
    )(
        conv, conv, tail8, tail8, conv_weight, conv_weight, bias, bias,
        step_b, cum_b, cum.T, skip_wide,
    )

    start_state = move_state(cache_state[0], all_slot, all_mask)

    final = pl.pallas_call(
        final_kernel,
        grid=(blocks,),
        in_specs=[
            pl.BlockSpec(memory_space=pltpu.SMEM),
            pl.BlockSpec((HB, HEAD_P, NSTATE), lambda b: (b, 0, 0)),
            pl.BlockSpec((HB, HEAD_P, NSTATE), lambda b: (b, 0, 0)),
        ],
        out_specs=pl.BlockSpec((HB, HEAD_P, NSTATE), lambda b: (b, 0, 0)),
        out_shape=jax.ShapeDtypeStruct((heads, HEAD_P, NSTATE), jnp.bfloat16),
        compiler_params=pltpu.CompilerParams(vmem_limit_bytes=VMEM),
        cost_estimate=pl.CostEstimate(flops=2_000_000, bytes_accessed=8_000_000, transcendentals=0),
    )(end_decay, add, start_state)

    owned = move_state(final, inverse, jnp.ones((n,), jnp.int32))

    y = pl.pallas_call(
        prefix_kernel,
        grid=(blocks,),
        in_specs=[
            pl.BlockSpec(memory_space=pltpu.SMEM),
            pl.BlockSpec((steps, HBW), lambda b: (0, b)),
            pl.BlockSpec((steps, NSTATE), lambda b: (0, b // BLOCKS)),
            pl.BlockSpec((1, steps, HB), lambda b: (b, 0, 0)),
            pl.BlockSpec((HB, HEAD_P, NSTATE), lambda b: (b, 0, 0)),
        ],
        out_specs=pl.BlockSpec((steps, HBW), lambda b: (0, b)),
        out_shape=jax.ShapeDtypeStruct((steps, heads * HEAD_P), jnp.bfloat16),
        compiler_params=pltpu.CompilerParams(vmem_limit_bytes=VMEM),
        cost_estimate=pl.CostEstimate(
            flops=6_000_000_000, bytes_accessed=9_000_000, transcendentals=100_000
        ),
    )(suffix_len, y_part, c_rows, cum_b, start_state)
    return y[None], owned[None], out_tail


def solution(mesh):
    placed = (
        P(("groups", "cache"), None, ("mp", "sub")),
        P(("groups", "cache"), None, ("mp", "sub")),
        P(None, ("mp", "sub")),
        P(("mp", "sub")),
        P(("mp", "sub")),
        P(("mp", "sub")),
        P(("mp", "sub")),
        P(("groups", "cache"), ("mp", "sub"), None, None),
        P(("groups", "cache"), None, ("mp", "sub")),
        P(("groups", "cache")),
        P(("groups", "cache")),
        P(("groups", "cache")),
        P(("groups", "cache")),
    )
    return jax.shard_map(
        per_device,
        mesh=mesh,
        in_specs=placed,
        out_specs=(
            P(("groups", "cache"), None, ("mp", "sub")),
            P(("groups", "cache"), ("mp", "sub"), None, None),
            P(("groups", "cache"), None, ("mp", "sub")),
        ),
        check_vma=False,
    )
```

time: 425 us -> 247 us (0.58); the launches traced: 418 us -> 246 us
  other arithmetic: 130 us -> 5.27 us
  local copies, waits for them, and re-layouts: 111 us -> 13.2 us
  waiting for transfers between devices: 50.9 us -> 133 us
  Pallas kernels: 0 us -> 58.8 us
  blocking collectives: 55.2 us -> 14.9 us
  matrix products: 38.8 us -> 0 us
  starting transfers between devices: 27.2 us -> 14.7 us
    all_to_all x6 -> x4, waiting for transfers between devices: 50.9 us -> 133 us  [the longest x2 87.5 us: move_state(): lax.all_to_all(pieces, 'cache', split_axis=0, concat_axis=0, tiled=True)]
    pallas_call x0 -> x5, Pallas kernels: none -> 58.8 us  [the longest x1 32.1 us: per_device(): pl.pallas_call(scan_kernel, grid=(groups_here, BLOCKS), in_specs=[xs(step...]
    all_gather x1 -> x0, blocking collectives: 47 us -> none  [per_device(): tails_whole = lax.all_gather(tail_flat, 'cache', axis=0, tiled=True)]
    all_to_all x6 -> x0, other arithmetic: 46.3 us -> none  [the longest x3 30.4 us: per_device(): lax.all_to_all(ordered_state, 'cache', split_axis=0, concat_axis=1, tiled...]
    unnamed x70 -> x19, local copies, waits for them, and re-layouts: 48 us -> 4.8 us
    unnamed x5 -> x0, other arithmetic: 39.5 us -> none
    dot_general x5 -> x0, matrix products: 38.8 us -> none  [the longest x1 19.8 us: conv_and_scan(): jnp.einsum('ijgk,jgkp->igkp', weighted, x_scaled, precision=highest)]
    select_n x4 -> x1, other arithmetic: 17 us -> 0.02 us  [per_device(): jnp.where(hit_mask[0] > 0, start_tail, jnp.zeros((), jnp.bfloat16))]
  transfers between devices with their start and end apart: 6 -> 4, of which waited for: 2 -> 4; matrix products, arithmetic and copies ran while one was open for 48% -> 5% of each run, Pallas kernels for 0% -> 18%
where the time goes in v1:
time: 247 us; the launch traced here: 246 us
  waiting for transfers between devices  133 us (54%)
  Pallas kernels  58.8 us (24%)
  blocking collectives  14.9 us (6%)
  starting transfers between devices  14.7 us (6%)
  local copies, waits for them, and re-layouts  13.2 us (5%)
  between operations  5.37 us (2%)
  other arithmetic  5.27 us (2%)
    all_to_all x2, waiting for transfers between devices, move_state(): lax.all_to_all(pieces, 'cache', split_axis=0, concat_axis=0, tiled=True)  87.5 us
    all_to_all x2, waiting for transfers between devices, move_state(): lax.all_to_all(chosen, 'cache', split_axis=0, concat_axis=0, tiled=True)  45.8 us
    pallas_call x1, Pallas kernels, per_device(): pl.pallas_call(scan_kernel, grid=(groups_here, BLOCKS), in_specs=[xs(step...  32.1 us
    all_to_all x1, blocking collectives, per_device(): lax.all_to_all(jnp.broadcast_to(row[None], (n,) + row.shape), 'cache', sp...  14.9 us
    pallas_call x1, Pallas kernels, per_device(): pl.pallas_call(prefix_kernel, grid=(blocks,), in_specs=[pl.BlockSpec(memo...  11.1 us
    pallas_call x2, Pallas kernels, choose(): pl.pallas_call(choose_kernel, grid_spec=pltpu.PrefetchScalarGridSpec(num_...  9.07 us
    all_to_all x2, starting transfers between devices, move_state(): lax.all_to_all(pieces, 'cache', split_axis=0, concat_axis=0, tiled=True)  7.36 us
    all_to_all x2, starting transfers between devices, move_state(): lax.all_to_all(chosen, 'cache', split_axis=0, concat_axis=0, tiled=True)  7.35 us
  transfers between devices with their start and end apart: 4, of which 4 were waited for; matrix products, arithmetic and copies ran while one was open for 5% of the time, Pallas kernels for 18%

profile of v1, /device:TPU:0, one launch (start us, length us, event | category | flops | bytes accessed | tf_op | source)
XLA Modules:
  0.0 245.6 jit_solution(3992474015388537239)
XLA Ops:
  3.2 0.8 reshape.78
  4.1 1.0 constant_dynamic-slice_fusion.1
  5.2 14.9 %all_to_all.25 = bf16[4,241,128]{2,1,0:T(8,128)(2,1)} all-to-all(bf16[4,241,128]{2,1,0:T(8,128)(2,1)S(1)} %broadcast_in_dim.32), channel_id=1, replica_groups=mesh['groups'=2,'cache'=4,'mp'=2,'sub'=2] {'cache'}, dimensions={0} | all-to-all | bytes 493568 | tf_op jit(solution)/shard_map/all_to_all | solution.py:151
  20.1 3.8 %all-to-all-start.1 = ((bf16[4,16,64,256]{3,2,1,0:T(8,128)(2,1)}), bf16[4,16,64,256]{3,2,1,0:T(8,128)(2,1)S(1)}, u32[]{:S(2)}, u32[]{:S(2)}) async-start(bf16[4,16,64,256]{3,2,1,0:T(8,128)(2,1)} %bitcast.55), calls=%async_computation.1 | async-start | bytes 4194304 | tf_op jit(solution)/shard_map/all_to_all | solution.py:121
  24.1 0.7 reshape_reshape.3.skip_ref
  24.9 0.6 reduce-window.6
  26.3 0.7 fusion.6
  27.0 1.4 copy.32
  28.7 0.7 slice_convert_fusion
  29.4 0.8 slice_reduce_fusion.1
  30.2 40.5 %all-to-all-done.1.in_ref = bf16[4,16,64,256]{3,2,1,0:T(8,128)(2,1)S(1)} async-done(((bf16[4,16,64,256]{3,2,1,0:T(8,128)(2,1)}), bf16[4,16,64,256]{3,2,1,0:T(8,128)(2,1)S(1)}, u32[]{:S(2)}, u32[]{:S(2)}) %all-to-all-start.1) | async-done | bytes 2097184 | tf_op jit(solution)/shard_map/all_to_all | solution.py:121
  70.7 1.3 copy-done
  72.1 4.5 %shard_map.149 = bf16[4,16,64,256]{3,2,1,0:T(8,128)(2,1)} custom-call(s32[4]{0:T(128)} %get-tuple-element.11.slot_ref, s32[4]{0:T(128)} %get-tuple-element.10.mask_ref, bf16[4,16,64,256]{3,2,1,0:T(8,128)(2,1)} %copy-done), custom_call_target="tpu_custom_call" | custom-call | bytes 4194304 | tf_op jit(solution)/shard_map/pallas_call | solution.py:104
  76.6 3.6 %all-to-all-start.2 = ((bf16[4,16,64,256]{3,2,1,0:T(8,128)(2,1)}), bf16[4,16,64,256]{3,2,1,0:T(8,128)(2,1)S(1)}, u32[]{:S(2)}, u32[]{:S(2)}) async-start(bf16[4,16,64,256]{3,2,1,0:T(8,128)(2,1)} %shard_map.149), calls=%async_computation.2 | async-start | bytes 4194304 | tf_op jit(solution)/shard_map/all_to_all | solution.py:123
  80.2 0.8 fusion.3.decay_ref
  81.0 1.6 multiply_bitcast_fusion.step_ref
  82.7 0.7 pad_convert_fusion.tailx_ref.tailbc_ref
  83.3 32.1 %shard_map.148 = (f32[256,4096]{1,0:T(8,128)}, f32[256,512]{1,0:T(8,128)}, f32[64,64,256]{2,1,0:T(8,128)}) custom-call(bf16[256,5120]{1,0:T(8,128)(2,1)} %bitcast.59, bf16[256,5120]{1,0:T(8,128)(2,1)} %bitcast.60, f32[8,5120]{1,0:T(8,128)} %pad_convert_fusion.tailx_ref.tailbc_ref, f32[8,5120]{1,0:T(8,128)} %pad_convert_fusion.tailx_ref.tailbc_ref, ...), custom_call_target="tpu_custom_call" | custom-call | flops 20000000000 | bytes 12000000 | tf_op jit(solution)/shard_map/pallas_call | solution.py:186
  115.4 12.4 %all-to-all-done.2 = bf16[4,16,64,256]{3,2,1,0:T(8,128)(2,1)S(1)} async-done(((bf16[4,16,64,256]{3,2,1,0:T(8,128)(2,1)}), bf16[4,16,64,256]{3,2,1,0:T(8,128)(2,1)S(1)}, u32[]{:S(2)}, u32[]{:S(2)}) %all-to-all-start.2) | async-done | bytes 2097184 | tf_op jit(solution)/shard_map/all_to_all | solution.py:123
  127.9 1.3 copy-done.2
  129.2 6.6 %shard_map.151 = bf16[64,64,256]{2,1,0:T(8,128)(2,1)} custom-call(f32[64]{0:T(128)} %fusion.3.decay_ref, f32[64,64,256]{2,1,0:T(8,128)} %get-tuple-element.8.add_ref, bf16[64,64,256]{2,1,0:T(8,128)(2,1)} %bitcast.52), custom_call_target="tpu_custom_call" | custom-call | flops 2000000 | bytes 8000000 | tf_op jit(solution)/shard_map/pallas_call | solution.py:221
  135.8 3.6 %all-to-all-start.3 = ((bf16[4,16,64,256]{3,2,1,0:T(8,128)(2,1)}), bf16[4,16,64,256]{3,2,1,0:T(8,128)(2,1)S(1)}, u32[]{:S(2)}, u32[]{:S(2)}) async-start(bf16[4,16,64,256]{3,2,1,0:T(8,128)(2,1)} %bitcast.54), calls=%async_computation.3 | async-start | bytes 4194304 | tf_op jit(solution)/shard_map/all_to_all | solution.py:121
  139.4 0.6 select_reduce_fusion.slot_ref
  140.0 47.0 %all-to-all-done.3.in_ref = bf16[4,16,64,256]{3,2,1,0:T(8,128)(2,1)S(1)} async-done(((bf16[4,16,64,256]{3,2,1,0:T(8,128)(2,1)}), bf16[4,16,64,256]{3,2,1,0:T(8,128)(2,1)S(1)}, u32[]{:S(2)}, u32[]{:S(2)}) %all-to-all-start.3) | async-done | bytes 2097184 | tf_op jit(solution)/shard_map/all_to_all | solution.py:121
  187.6 0.8 copy-done.1
  188.4 4.5 %shard_map.152 = bf16[4,16,64,256]{3,2,1,0:T(8,128)(2,1)} custom-call(s32[4]{0:T(128)} %select_reduce_fusion.slot_ref, s32[4]{0:T(128)} %broadcast_1_mask_ref.2.mask_ref, bf16[4,16,64,256]{3,2,1,0:T(8,128)(2,1)} %copy-done.1), custom_call_target="tpu_custom_call" | custom-call | bytes 4194304 | tf_op jit(solution)/shard_map/pallas_call | solution.py:104
  192.9 3.7 %all-to-all-start.4 = ((bf16[4,16,64,256]{3,2,1,0:T(8,128)(2,1)}), bf16[4,16,64,256]{3,2,1,0:T(8,128)(2,1)S(1)}, u32[]{:S(2)}, u32[]{:S(2)}) async-start(bf16[4,16,64,256]{3,2,1,0:T(8,128)(2,1)} %shard_map.152), calls=%async_computation.4 | async-start | bytes 4194304 | tf_op jit(solution)/shard_map/all_to_all | solution.py:123
  196.7 0.6 dynamic_slice.15
  199.2 0.6 reshape.87
  199.9 11.1 %shard_map.150 = bf16[256,4096]{1,0:T(8,128)(2,1)} custom-call(s32[1]{0:T(128)} %copy.44.len_ref, f32[256,4096]{1,0:T(8,128)} %get-tuple-element.6.y_ref, f32[256,512]{1,0:T(8,128)} %get-tuple-element.7.c_ref, f32[8,256,8]{2,1,0:T(8,128)} %bitcast.57, bf16[64,64,256]{2,1,0:T(8,128)(2,1)} %bitcast.53), custom_call_target="tpu_custom_call" | custom-call | flops 6000000000 | bytes 9000000 | tf_op jit(solution)/shard_map/pallas_call | solution.py:237
  211.0 33.4 %all-to-all-done.4 = bf16[4,16,64,256]{3,2,1,0:T(8,128)(2,1)S(1)} async-done(((bf16[4,16,64,256]{3,2,1,0:T(8,128)(2,1)}), bf16[4,16,64,256]{3,2,1,0:T(8,128)(2,1)S(1)}, u32[]{:S(2)}, u32[]{:S(2)}) %all-to-all-start.4) | async-done | bytes 2097184 | tf_op jit(solution)/shard_map/all_to_all | solution.py:123
  244.3 1.3 copy.46
  (35 shorter events, 2.1 us)
Async XLA Ops:
  20.1 3.8 %copy-start.5 = (f32[64]{0:T(128)S(1)}, f32[64]{0:T(128)}, u32[]{:S(2)}) copy-start(f32[64]{0:T(128)} %param.17) | copy-start | bytes 772
  20.1 3.9 %copy-start.6 = (f32[64]{0:T(128)S(1)}, f32[64]{0:T(128)}, u32[]{:S(2)}) copy-start(f32[64]{0:T(128)} %param.19) | copy-start | bytes 772
  20.1 4.6 %copy-start.8 = (f32[64]{0:T(128)S(1)}, f32[64]{0:T(128)}, u32[]{:S(2)}) copy-start(f32[64]{0:T(128)} %param.18) | copy-start | bytes 772
  20.1 4.7 %copy-start.4 = (f32[1,256,64]{1,2,0:T(8,128)S(1)}, f32[1,256,64]{1,2,0:T(8,128)}, u32[]{:S(2)}) copy-start(f32[1,256,64]{1,2,0:T(8,128)} %param.14) | copy-start | bytes 196612
  20.1 50.6 %all-to-all-start.1 = ((bf16[4,16,64,256]{3,2,1,0:T(8,128)(2,1)}), bf16[4,16,64,256]{3,2,1,0:T(8,128)(2,1)S(1)}, u32[]{:S(2)}, u32[]{:S(2)}) async-start(bf16[4,16,64,256]{3,2,1,0:T(8,128)(2,1)} %bitcast.55), calls=%async_computation.1 | async-start | bytes 4194304 | tf_op jit(solution)/shard_map/all_to_all | solution.py:121
  70.7 1.3 copy-start
  76.6 51.3 %all-to-all-start.2 = ((bf16[4,16,64,256]{3,2,1,0:T(8,128)(2,1)}), bf16[4,16,64,256]{3,2,1,0:T(8,128)(2,1)S(1)}, u32[]{:S(2)}, u32[]{:S(2)}) async-start(bf16[4,16,64,256]{3,2,1,0:T(8,128)(2,1)} %shard_map.149), calls=%async_computation.2 | async-start | bytes 4194304 | tf_op jit(solution)/shard_map/all_to_all | solution.py:123
  80.2 2.4 copy-start.3
  127.9 1.3 copy-start.2
  135.8 51.3 %all-to-all-start.3 = ((bf16[4,16,64,256]{3,2,1,0:T(8,128)(2,1)}), bf16[4,16,64,256]{3,2,1,0:T(8,128)(2,1)S(1)}, u32[]{:S(2)}, u32[]{:S(2)}) async-start(bf16[4,16,64,256]{3,2,1,0:T(8,128)(2,1)} %bitcast.54), calls=%async_computation.3 | async-start | bytes 4194304 | tf_op jit(solution)/shard_map/all_to_all | solution.py:121
  187.0 1.3 copy-start.1
  192.9 3.8 %copy-start.7 = (s32[4]{0:T(128)S(1)}, s32[4]{0:T(128)}, u32[]{:S(2)}) copy-start(s32[4]{0:T(128)} %select_reduce_fusion.slot_ref) | copy-start | bytes 52
  192.9 51.4 %all-to-all-start.4 = ((bf16[4,16,64,256]{3,2,1,0:T(8,128)(2,1)}), bf16[4,16,64,256]{3,2,1,0:T(8,128)(2,1)S(1)}, u32[]{:S(2)}, u32[]{:S(2)}) async-start(bf16[4,16,64,256]{3,2,1,0:T(8,128)(2,1)} %shard_map.152), calls=%async_computation.4 | async-start | bytes 4194304 | tf_op jit(solution)/shard_map/all_to_all | solution.py:123

commit v2 on v1

--- a/solution.py
+++ b/solution.py
@@ -1,3 +1,5 @@
+import functools
+
 import jax
 import jax.numpy as jnp
 from jax import lax
@@ -17,6 +19,9 @@
 
 highest = lax.Precision.HIGHEST
 f32 = jnp.float32
+MESH = pl.DeviceIdType.MESH
+LINE = 4
+CHUNKS = 16
 
 
 def dot(a, b, dims):
@@ -125,6 +130,155 @@
     )
 
 
+def relay_kernel(
+    n, chunks, pick_ref, own_ref, out_ref,
+    right_in, left_in, right_out, left_out, send_r, recv_r, send_l, recv_l,
+):
+    me = lax.axis_index("cache")
+    per = own_ref.shape[0] // chunks
+    first, last = me == 0, me == n - 1
+    barrier = pltpu.get_barrier_semaphore()
+
+    @pl.when(jnp.logical_not(first))
+    def _():
+        pl.semaphore_signal(barrier, inc=1, device_id={"cache": me - 1}, device_id_type=MESH)
+
+    @pl.when(jnp.logical_not(last))
+    def _():
+        pl.semaphore_signal(barrier, inc=1, device_id={"cache": me + 1}, device_id_type=MESH)
+
+    @pl.when(jnp.logical_or(first, last))
+    def _():
+        pl.semaphore_wait(barrier, 1)
+
+    @pl.when(jnp.logical_not(jnp.logical_or(first, last)))
+    def _():
+        pl.semaphore_wait(barrier, 2)
+
+    def go_right(c, src):
+        return pltpu.make_async_remote_copy(
+            src_ref=src.at[pl.ds(c * per, per)], dst_ref=right_in.at[pl.ds(c * per, per)],
+            send_sem=send_r.at[c], recv_sem=recv_r.at[c],
+            device_id={"cache": lax.rem(me + 1, n)}, device_id_type=MESH,
+        )
+
+    def go_left(c, src):
+        return pltpu.make_async_remote_copy(
+            src_ref=src.at[pl.ds(c * per, per)], dst_ref=left_in.at[pl.ds(c * per, per)],
+            send_sem=send_l.at[c], recv_sem=recv_l.at[c],
+            device_id={"cache": lax.rem(me + n - 1, n)}, device_id_type=MESH,
+        )
+
+    @pl.when(first)
+    def _():
+        @pl.loop(0, chunks)
+        def _(c):
+            go_right(c, own_ref).start()
+
+    @pl.when(last)
+    def _():
+        @pl.loop(0, chunks)
+        def _(c):
+            go_left(c, own_ref).start()
+
+    @pl.loop(0, chunks + n - 1)
+    def _(s):
+        cr = s - me
+        cl = s - (n - 1 - me)
+
+        @pl.when(jnp.logical_and(jnp.logical_not(first), jnp.logical_and(cr >= 0, cr < chunks)))
+        def _():
+            go_right(cr, own_ref).wait_recv()
+
+            @pl.when(jnp.logical_not(last))
+            def _():
+                at = pl.ds(cr * per, per)
+                right_out[at] = jnp.where(pick_ref[0] > 0, own_ref[at], right_in[at])
+                go_right(cr, right_out).start()
+
+        @pl.when(jnp.logical_and(jnp.logical_not(last), jnp.logical_and(cl >= 0, cl < chunks)))
+        def _():
+            go_left(cl, own_ref).wait_recv()
+
+            @pl.when(jnp.logical_not(first))
+            def _():
+                at = pl.ds(cl * per, per)
+                left_out[at] = jnp.where(pick_ref[1] > 0, own_ref[at], left_in[at])
+                go_left(cl, left_out).start()
+
+    def result(low, high):
+        @pl.loop(0, chunks)
+        def _(c):
+            at = pl.ds(c * per, per)
+            value = own_ref[at]
+            if low:
+                value = jnp.where(pick_ref[2] > 0, right_in[at], value)
+            if high:
+                value = jnp.where(pick_ref[3] > 0, left_in[at], value)
+            out_ref[at] = jnp.where(pick_ref[4] > 0, value, jnp.zeros_like(value))
+
+    @pl.when(first)
+    def _():
+        result(False, True)
+
+    @pl.when(last)
+    def _():
+        result(True, False)
+
+    @pl.when(jnp.logical_not(jnp.logical_or(first, last)))
+    def _():
+        result(True, True)
+
+    @pl.when(jnp.logical_not(last))
+    def _():
+        @pl.loop(0, chunks)
+        def _(c):
+            go_right(c, own_ref).wait_send()
+
+    @pl.when(jnp.logical_not(first))
+    def _():
+        @pl.loop(0, chunks)
+        def _(c):
+            go_left(c, own_ref).wait_send()
+
+
+def relay(state, picks):
+    n = lax.axis_size("cache")
+    chunks = min(CHUNKS, state.shape[0])
+    vmem = pl.BlockSpec(memory_space=pltpu.VMEM)
+    return pl.pallas_call(
+        functools.partial(relay_kernel, n, chunks),
+        in_specs=[pl.BlockSpec(memory_space=pltpu.SMEM), vmem],
+        out_specs=vmem,
+        out_shape=jax.ShapeDtypeStruct(state.shape, state.dtype),
+        scratch_shapes=[pltpu.VMEM(state.shape, state.dtype)] * 4
+        + [pltpu.SemaphoreType.DMA((chunks,))] * 4,
+        compiler_params=pltpu.CompilerParams(
+            collective_id=0, has_side_effects=True, vmem_limit_bytes=32 * 1024 * 1024
+        ),
+        cost_estimate=pl.CostEstimate(
+            flops=0, bytes_accessed=100_000_000, transcendentals=0
+        ),
+    )(picks, state)
+
+
+def relay_plan(slot, mask):
+    n = lax.axis_size("cache")
+    me = lax.axis_index("cache")
+    ids = jnp.arange(n, dtype=jnp.int32)
+    wants = (slot[None, :] == ids[:, None]) & (mask[None, :] > 0)
+    right_of = ids[None, :] > ids[:, None]
+    right = jnp.any(wants[:, None, :] & right_of[None], axis=2) & (ids[:, None] <= ids[None, :])
+    left = jnp.any(wants[:, None, :] & right_of.T[None], axis=2) & (ids[:, None] >= ids[None, :])
+    most = jnp.maximum(
+        jnp.max(jnp.sum(right.astype(jnp.int32), axis=0)),
+        jnp.max(jnp.sum(left.astype(jnp.int32), axis=0)),
+    )
+    mine = slot[me]
+    picks = jnp.stack([right[me, me], left[me, me], mine < me, mine > me, mask[me] > 0])
+    return picks.astype(jnp.int32), most
+
+
 def per_device(
     conv_input, dt_raw, conv_weight, conv_bias, dt_bias, a_log, d_skip,
     cache_state, cache_tail, hit_slot, hit_mask, suffix_len, write_slot,
@@ -148,10 +302,20 @@
         ],
         axis=0,
     )
-    rows = lax.all_to_all(
-        jnp.broadcast_to(row[None], (n,) + row.shape), "cache", split_axis=0, concat_axis=0,
-        tiled=True,
-    )
+    if n <= LINE:
+        steps_by = [row] + [
+            lax.ppermute(row, "cache", [(i, (i + shift) % n) for i in range(n)])
+            for shift in range(1, n)
+        ]
+        came = jnp.stack(steps_by)
+        rows = jnp.stack(
+            [lax.dynamic_index_in_dim(came, (me - i) % n, 0, keepdims=False) for i in range(n)]
+        )
+    else:
+        rows = lax.all_to_all(
+            jnp.broadcast_to(row[None], (n,) + row.shape), "cache", split_axis=0, concat_axis=0,
+            tiled=True,
+        )
     table = rows[:, -1, :3].astype(jnp.int32)
     all_slot, all_mask, all_write = table[:, 0], table[:, 1], table[:, 2]
     ids = jnp.arange(n, dtype=jnp.int32)
@@ -232,25 +396,42 @@
         cost_estimate=pl.CostEstimate(flops=2_000_000, bytes_accessed=8_000_000, transcendentals=0),
     )(end_decay, add, start_state)
 
-    owned = move_state(final, inverse, jnp.ones((n,), jnp.int32))
-
-    y = pl.pallas_call(
-        prefix_kernel,
-        grid=(blocks,),
-        in_specs=[
-            pl.BlockSpec(memory_space=pltpu.SMEM),
-            pl.BlockSpec((steps, HBW), lambda b: (0, b)),
-            pl.BlockSpec((steps, NSTATE), lambda b: (0, b // BLOCKS)),
-            pl.BlockSpec((1, steps, HB), lambda b: (b, 0, 0)),
-            pl.BlockSpec((HB, HEAD_P, NSTATE), lambda b: (b, 0, 0)),
-        ],
-        out_specs=pl.BlockSpec((steps, HBW), lambda b: (0, b)),
-        out_shape=jax.ShapeDtypeStruct((steps, heads * HEAD_P), jnp.bfloat16),
-        compiler_params=pltpu.CompilerParams(vmem_limit_bytes=VMEM),
-        cost_estimate=pl.CostEstimate(
-            flops=6_000_000_000, bytes_accessed=9_000_000, transcendentals=100_000
-        ),
-    )(suffix_len, y_part, c_rows, cum_b, start_state)
+    def prefix(start):
+        return pl.pallas_call(
+            prefix_kernel,
+            grid=(blocks,),
+            in_specs=[
+                pl.BlockSpec(memory_space=pltpu.SMEM),
+                pl.BlockSpec((steps, HBW), lambda b: (0, b)),
+                pl.BlockSpec((steps, NSTATE), lambda b: (0, b // BLOCKS)),
+                pl.BlockSpec((1, steps, HB), lambda b: (b, 0, 0)),
+                pl.BlockSpec((HB, HEAD_P, NSTATE), lambda b: (b, 0, 0)),
+            ],
+            out_specs=pl.BlockSpec((steps, HBW), lambda b: (0, b)),
+            out_shape=jax.ShapeDtypeStruct((steps, heads * HEAD_P), jnp.bfloat16),
+            compiler_params=pltpu.CompilerParams(vmem_limit_bytes=VMEM),
+            cost_estimate=pl.CostEstimate(
+                flops=6_000_000_000, bytes_accessed=9_000_000, transcendentals=100_000
+            ),
+        )(suffix_len, y_part, c_rows, cum_b, start)
+
+    def two_phase(final, start):
+        return move_state(final, inverse, ones), prefix(start)
+
+    def along_line(final, start):
+        return relay(final, picks), prefix(start)
+
+    ones = jnp.ones((n,), jnp.int32)
+    if n <= LINE:
+        picks, most = relay_plan(inverse, ones)
+        count = lax.axis_size("groups")
+        here = most
+        for shift in range(1, count):
+            ring = [(i, (i + shift) % count) for i in range(count)]
+            most = jnp.maximum(most, lax.ppermute(here, "groups", ring))
+        owned, y = lax.cond(most <= 1, along_line, two_phase, final, start_state)
+    else:
+        owned, y = two_phase(final, start_state)
     return y[None], owned[None], out_tail
 
 

time: 247 us -> 205 us (0.83)
  waiting for transfers between devices: 133 us -> 38 us
  Pallas kernels: 58.8 us -> 116 us
  blocking collectives: 14.9 us -> 0 us
  starting transfers between devices: 14.7 us -> 18 us
  between operations: 5.37 us -> 8.54 us
  other arithmetic: 5.27 us -> 8.2 us
    all_to_all x2 -> x1, waiting for transfers between devices: 87.5 us -> 0.01 us  [move_state(): lax.all_to_all(pieces, 'cache', split_axis=0, concat_axis=0, tiled=True)]
    pallas_call x1 -> x2, Pallas kernels: 11.1 us -> 74.1 us  [the longest x1 62.8 us: relay(): pl.pallas_call(functools.partial(relay_kernel, n, chunks), in_specs=[pl.B...]
    all_to_all x2 -> x1, waiting for transfers between devices: 45.8 us -> 3.54 us  [move_state(): lax.all_to_all(chosen, 'cache', split_axis=0, concat_axis=0, tiled=True)]
    ppermute x0 -> x4, waiting for transfers between devices: none -> 34.5 us  [the longest x3 34.5 us: per_device(): lax.ppermute(row, 'cache', [(i, (i + shift) % n) for i in range(n)])]
    all_to_all x1 -> x0, blocking collectives: 14.9 us -> none  [per_device(): lax.all_to_all(jnp.broadcast_to(row[None], (n,) + row.shape), 'cache', sp...]
    ppermute x0 -> x4, starting transfers between devices: none -> 7.83 us  [the longest x3 4.95 us: per_device(): lax.ppermute(row, 'cache', [(i, (i + shift) % n) for i in range(n)])]
    pallas_call x2 -> x1, Pallas kernels: 9.07 us -> 4.28 us  [choose(): pl.pallas_call(choose_kernel, grid_spec=pltpu.PrefetchScalarGridSpec(num_...]
    all_to_all x2 -> x1, starting transfers between devices: 7.35 us -> 3.74 us  [move_state(): lax.all_to_all(chosen, 'cache', split_axis=0, concat_axis=0, tiled=True)]
  transfers between devices with their start and end apart: 4 -> 6, of which waited for: 4 -> 4; matrix products, arithmetic and copies ran while one was open for 5% -> 10% of each run, Pallas kernels for 18% -> 16%
where the time goes in v2:
time: 205 us; the launch traced here: 204 us
  Pallas kernels  116 us (57%)
  waiting for transfers between devices  38 us (19%)
  starting transfers between devices  18 us (9%)
  local copies, waits for them, and re-layouts  15.6 us (8%)
  between operations  8.54 us (4%)
  other arithmetic  8.2 us (4%)
    pallas_call x1, Pallas kernels, relay(): pl.pallas_call(functools.partial(relay_kernel, n, chunks), in_specs=[pl.B...  62.8 us
    ppermute x3, waiting for transfers between devices, per_device(): lax.ppermute(row, 'cache', [(i, (i + shift) % n) for i in range(n)])  34.5 us
    pallas_call x1, Pallas kernels, per_device(): pl.pallas_call(scan_kernel, grid=(groups_here, BLOCKS), in_specs=[xs(step...  32 us
    pallas_call x1, Pallas kernels, prefix(): pl.pallas_call(prefix_kernel, grid=(blocks,), in_specs=[pl.BlockSpec(memo...  11.3 us
    all_to_all x1, starting transfers between devices, move_state(): lax.all_to_all(pieces, 'cache', split_axis=0, concat_axis=0, tiled=True)  6.46 us
    pallas_call x1, Pallas kernels, per_device(): pl.pallas_call(final_kernel, grid=(blocks,), in_specs=[pl.BlockSpec(memor...  5.17 us
    ppermute x3, starting transfers between devices, per_device(): lax.ppermute(row, 'cache', [(i, (i + shift) % n) for i in range(n)])  4.95 us
    pallas_call x1, Pallas kernels, choose(): pl.pallas_call(choose_kernel, grid_spec=pltpu.PrefetchScalarGridSpec(num_...  4.28 us
  transfers between devices with their start and end apart: 6, of which 4 were waited for; matrix products, arithmetic and copies ran while one was open for 10% of the time, Pallas kernels for 16%

profile of v2, /device:TPU:0, one launch (start us, length us, event | category | flops | bytes accessed | tf_op | source)
XLA Modules:
  0.0 204.1 jit_solution(15539929808648807369)
XLA Ops:
  0.7 6.5 %all-to-all-start.2 = ((bf16[4,16,64,256]{3,2,1,0:T(8,128)(2,1)}), bf16[4,16,64,256]{3,2,1,0:T(8,128)(2,1)S(1)}, u32[]{:S(2)}, u32[]{:S(2)}) async-start(bf16[4,16,64,256]{3,2,1,0:T(8,128)(2,1)} %bitcast.68), calls=%async_computation.2 | async-start | bytes 4194304 | tf_op jit(solution)/shard_map/all_to_all | solution.py:126
  7.8 1.0 constant_dynamic-slice_fusion.4
  10.9 0.6 fusion.16
  11.5 3.8 %collective-permute-start.2 = (bf16[241,128]{1,0:T(8,128)(2,1)}, bf16[241,128]{1,0:T(8,128)(2,1)}, u32[]{:S(2)}, u32[]{:S(2)}) collective-permute-start(bf16[241,128]{1,0:T(8,128)(2,1)} %get-tuple-element.74), channel_id=1, source_target_pairs={{0,12},{4,0},{8,4},{12,8},{1,13},{5,1},{9,5},{13,9},{2,14},{6,2},{... | collective-permute-start | bytes 185096 | tf_op jit(solution)/shard_map/ppermute | solution.py:307
  15.3 1.1 collective-permute-start.1
  17.5 0.7 copy_bitcast_fusion
  18.3 1.3 copy.36
  20.5 1.3 broadcast_in_dim.64
  21.8 1.4 reshape_reshape.3.skip_ref
  23.3 0.8 fusion.3.decay_ref
  24.0 2.4 %multiply_bitcast_fusion.step_ref = f32[8,256,8]{2,1,0:T(8,128)} fusion(pred[256,8,8]{2,0,1:T(8,128)(4,1)S(1)} %copy.34, f32[256,8,8]{2,0,1:T(8,128)S(1)} %copy.35, f32[256]{0:T(256)} %copy-done.7), kind=kLoop, calls=%fused_computation | loop fusion | flops 98304 | bytes 148480 | tf_op jit(solution)/shard_map/transpose | solution.py:335
  26.4 17.2 %collective-permute-done.2 = bf16[241,128]{1,0:T(8,128)(2,1)} collective-permute-done((bf16[241,128]{1,0:T(8,128)(2,1)}, bf16[241,128]{1,0:T(8,128)(2,1)}, u32[]{:S(2)}, u32[]{:S(2)}) %collective-permute-start.2) | collective-permute-done | bytes 61728 | tf_op jit(solution)/shard_map/ppermute | solution.py:307
  43.7 4.9 %collective-permute-done = bf16[241,128]{1,0:T(8,128)(2,1)} collective-permute-done((bf16[241,128]{1,0:T(8,128)(2,1)}, bf16[241,128]{1,0:T(8,128)(2,1)}, u32[]{:S(2)}, u32[]{:S(2)}) %collective-permute-start) | collective-permute-done | bytes 61728 | tf_op jit(solution)/shard_map/ppermute | solution.py:307
  48.6 12.3 %collective-permute-done.1 = bf16[241,128]{1,0:T(8,128)(2,1)} collective-permute-done((bf16[241,128]{1,0:T(8,128)(2,1)}, bf16[241,128]{1,0:T(8,128)(2,1)}, u32[]{:S(2)}, u32[]{:S(2)}) %collective-permute-start.1) | collective-permute-done | bytes 61728 | tf_op jit(solution)/shard_map/ppermute | solution.py:307
  60.9 0.9 pad_maximum_fusion
  61.9 0.8 slice_reduce_fusion.1
  62.8 0.6 dynamic_slice.41
  65.3 1.3 copy-done
  66.6 4.3 %shard_map.149 = bf16[4,16,64,256]{3,2,1,0:T(8,128)(2,1)} custom-call(s32[4]{0:T(128)} %get-tuple-element.58.slot_ref, s32[4]{0:T(128)} %get-tuple-element.57.mask_ref, bf16[4,16,64,256]{3,2,1,0:T(8,128)(2,1)} %copy-done), custom_call_target="tpu_custom_call" | custom-call | bytes 4194304 | tf_op jit(solution)/shard_map/pallas_call | solution.py:109
  70.9 3.7 %all-to-all-start.3 = ((bf16[4,16,64,256]{3,2,1,0:T(8,128)(2,1)}), bf16[4,16,64,256]{3,2,1,0:T(8,128)(2,1)S(1)}, u32[]{:S(2)}, u32[]{:S(2)}) async-start(bf16[4,16,64,256]{3,2,1,0:T(8,128)(2,1)} %shard_map.149), calls=%async_computation.3 | async-start | bytes 4194304 | tf_op jit(solution)/shard_map/all_to_all | solution.py:128
  77.6 1.4 stack.39
  79.1 0.6 reduce_max.18
  81.6 2.9 %collective-permute-start.3 = (s32[]{:T(128)}, s32[]{:T(128)}, u32[]{:S(2)}, u32[]{:S(2)}) collective-permute-start(s32[]{:T(128)} %max.19), channel_id=1, source_target_pairs={{0,16},{16,0},{1,17},{17,1},{2,18},{18,2},{3,19},{19,3},{4,20},{20... | collective-permute-start | bytes 20 | tf_op jit(solution)/shard_map/ppermute | solution.py:431
  85.1 0.7 pad_convert_fusion.tailx_ref.tailbc_ref
  85.8 32.0 %shard_map.148 = (f32[256,4096]{1,0:T(8,128)}, f32[256,512]{1,0:T(8,128)}, f32[64,64,256]{2,1,0:T(8,128)}) custom-call(bf16[256,5120]{1,0:T(8,128)(2,1)} %bitcast.73, bf16[256,5120]{1,0:T(8,128)(2,1)} %bitcast.74, f32[8,5120]{1,0:T(8,128)} %pad_convert_fusion.tailx_ref.tailbc_ref, f32[8,5120]{1,0:T(8,128)} %pad_convert_fusion.tailx_ref.tailbc_ref, ...), custom_call_target="tpu_custom_call" | custom-call | flops 20000000000 | bytes 12000000 | tf_op jit(solution)/shard_map/pallas_call | solution.py:350
  118.5 3.5 %all-to-all-done.3 = bf16[4,16,64,256]{3,2,1,0:T(8,128)(2,1)S(1)} async-done(((bf16[4,16,64,256]{3,2,1,0:T(8,128)(2,1)}), bf16[4,16,64,256]{3,2,1,0:T(8,128)(2,1)S(1)}, u32[]{:S(2)}, u32[]{:S(2)}) %all-to-all-start.3) | async-done | bytes 2097184 | tf_op jit(solution)/shard_map/all_to_all | solution.py:128
  122.0 1.3 copy-done.2
  123.4 5.2 %shard_map.150 = bf16[64,64,256]{2,1,0:T(8,128)(2,1)S(1)} custom-call(f32[64]{0:T(128)} %fusion.3.decay_ref, f32[64,64,256]{2,1,0:T(8,128)} %get-tuple-element.52.add_ref, bf16[64,64,256]{2,1,0:T(8,128)(2,1)} %bitcast.65), custom_call_target="tpu_custom_call" | custom-call | flops 2000000 | bytes 8000000 | tf_op jit(solution)/shard_map/pallas_call | solution.py:385
  128.5 74.2 %conditional.1 = (bf16[1,64,64,256]{3,2,1,0:T(8,128)(2,1)S(1)}, bf16[1,256,4096]{2,1,0:T(8,128)(2,1)}) conditional(s32[]{:T(128)} %convert_element_type.39, (bf16[64,64,256]{2,1,0:T(8,128)(2,1)S(1)}, s32[4]{0:T(128)S(1)}, s32[1]{0:T(128)}, f32[256,4096]{1,0:T(8,128)}, f32[256,512]{1,0:T(8,128)}, /*index=5*/f32[8,256,8]{2,1,0:T(8,128)S(1)}, ...), branch_computations={%region_9.10_spmd, %region_10.11_spmd} | conditional | flops 6000000000 | bytes 127874472 | solution.py:432
  128.6 62.8 %branch_1_fun.2 = bf16[64,64,256]{2,1,0:T(8,128)(2,1)} custom-call(s32[5]{0:T(128)S(1)} %get-tuple-element.37.pick_ref, bf16[64,64,256]{2,1,0:T(8,128)(2,1)S(1)} %get-tuple-element.38.own_ref), custom_call_target="tpu_custom_call" | custom-call | bytes 100000000 | tf_op jit(solution)/shard_map/cond/branch_1_fun/pallas_call | solution.py:249
  191.4 11.3 %branch_1_fun.3 = bf16[256,4096]{1,0:T(8,128)(2,1)} custom-call(s32[1]{0:T(128)} %get-tuple-element.39.len_ref, f32[256,4096]{1,0:T(8,128)} %get-tuple-element.40.y_ref, f32[256,512]{1,0:T(8,128)S(1)} %copy-done.10, f32[8,256,8]{2,1,0:T(8,128)S(1)} %get-tuple-element.42.cum_ref, bf16[64,64,256]{2,1,0:T(8,128)(2,1)S(1)} %copy-done.3), custom_call_target="tpu_custom_call" | custom-call | flops 6000000000 | bytes 9000000 | tf_op jit(solution)/shard_map/cond/branch_1_fun/pallas_call | solution.py:400
  202.7 1.3 copy.54
  (53 shorter events, 5.2 us)
Async XLA Ops:
  0.6 10.1 %copy-start.6 = (bf16[1,3,5120]{2,1,0:T(4,128)(2,1)S(1)}, bf16[1,3,5120]{2,1,0:T(4,128)(2,1)}, u32[]{:S(2)}) copy-start(bf16[1,3,5120]{2,1,0:T(4,128)(2,1)} %param.23) | copy-start | bytes 92164
  0.6 15.8 %copy-start.8 = (f32[64]{0:T(128)S(1)}, f32[64]{0:T(128)}, u32[]{:S(2)}) copy-start(f32[64]{0:T(128)} %param.19) | copy-start | bytes 772
  0.7 15.9 %copy-start.9 = (f32[64]{0:T(128)S(1)}, f32[64]{0:T(128)}, u32[]{:S(2)}) copy-start(f32[64]{0:T(128)} %param.20) | copy-start | bytes 772
  0.7 15.9 %copy-start.5 = (f32[1,256,64]{1,2,0:T(8,128)S(1)}, f32[1,256,64]{1,2,0:T(8,128)}, u32[]{:S(2)}) copy-start(f32[1,256,64]{1,2,0:T(8,128)} %param.16) | copy-start | bytes 196612
  0.7 64.6 %all-to-all-start.2 = ((bf16[4,16,64,256]{3,2,1,0:T(8,128)(2,1)}), bf16[4,16,64,256]{3,2,1,0:T(8,128)(2,1)S(1)}, u32[]{:S(2)}, u32[]{:S(2)}) async-start(bf16[4,16,64,256]{3,2,1,0:T(8,128)(2,1)} %bitcast.68), calls=%async_computation.2 | async-start | bytes 4194304 | tf_op jit(solution)/shard_map/all_to_all | solution.py:126
  11.5 32.1 %collective-permute-start.2 = (bf16[241,128]{1,0:T(8,128)(2,1)}, bf16[241,128]{1,0:T(8,128)(2,1)}, u32[]{:S(2)}, u32[]{:S(2)}) collective-permute-start(bf16[241,128]{1,0:T(8,128)(2,1)} %get-tuple-element.74), channel_id=1, source_target_pairs={{0,12},{4,0},{8,4},{12,8},{1,13},{5,1},{9,5},{13,9},{2,14},{6,2},{... | collective-permute-start | bytes 185096 | tf_op jit(solution)/shard_map/ppermute | solution.py:307
  15.3 33.2 %collective-permute-start = (bf16[241,128]{1,0:T(8,128)(2,1)}, bf16[241,128]{1,0:T(8,128)(2,1)}, u32[]{:S(2)}, u32[]{:S(2)}) collective-permute-start(bf16[241,128]{1,0:T(8,128)(2,1)} %get-tuple-element.74), channel_id=1, source_target_pairs={{0,4},{4,8},{8,12},{12,0},{1,5},{5,9},{9,13},{13,1},{2,6},{6,10},{... | collective-permute-start | bytes 185096 | tf_op jit(solution)/shard_map/ppermute | solution.py:307
  15.3 45.5 %collective-permute-start.1 = (bf16[241,128]{1,0:T(8,128)(2,1)}, bf16[241,128]{1,0:T(8,128)(2,1)}, u32[]{:S(2)}, u32[]{:S(2)}) collective-permute-start(bf16[241,128]{1,0:T(8,128)(2,1)} %get-tuple-element.74), channel_id=1, source_target_pairs={{0,8},{4,12},{8,0},{12,4},{1,9},{5,13},{9,1},{13,5},{2,10},{6,14},... | collective-permute-start | bytes 185096 | tf_op jit(solution)/shard_map/ppermute | solution.py:307
  16.6 0.8 copy-start.7
  65.3 1.3 copy-start
  70.9 14.9 %copy-start.4 = (f32[256,8,8]{2,0,1:T(8,128)S(1)}, f32[256,8,8]{2,0,1:T(8,128)}, u32[]{:S(2)}) copy-start(f32[256,8,8]{2,0,1:T(8,128)} %copy.36) | copy-start | bytes 196612
  70.9 51.1 %all-to-all-start.3 = ((bf16[4,16,64,256]{3,2,1,0:T(8,128)(2,1)}), bf16[4,16,64,256]{3,2,1,0:T(8,128)(2,1)S(1)}, u32[]{:S(2)}, u32[]{:S(2)}) async-start(bf16[4,16,64,256]{3,2,1,0:T(8,128)(2,1)} %shard_map.149), calls=%async_computation.3 | async-start | bytes 4194304 | tf_op jit(solution)/shard_map/all_to_all | solution.py:128
  81.6 36.2 %collective-permute-start.3 = (s32[]{:T(128)}, s32[]{:T(128)}, u32[]{:S(2)}, u32[]{:S(2)}) collective-permute-start(s32[]{:T(128)} %max.19), channel_id=1, source_target_pairs={{0,16},{16,0},{1,17},{17,1},{2,18},{18,2},{3,19},{19,3},{4,20},{20... | collective-permute-start | bytes 20 | tf_op jit(solution)/shard_map/ppermute | solution.py:431
  122.0 1.3 copy-start.2
  128.6 62.8 %copy-start.3 = (bf16[64,64,256]{2,1,0:T(8,128)(2,1)S(1)}, bf16[64,64,256]{2,1,0:T(8,128)(2,1)}, u32[]{:S(2)}) copy-start(bf16[64,64,256]{2,1,0:T(8,128)(2,1)} %get-tuple-element.43.state_ref) | copy-start | bytes 6291460 | tf_op jit(solution)/shard_map/cond
  128.6 62.8 %copy-start.10 = (f32[256,512]{1,0:T(8,128)S(1)}, f32[256,512]{1,0:T(8,128)}, u32[]{:S(2)}) copy-start(f32[256,512]{1,0:T(8,128)} %get-tuple-element.41.c_ref) | copy-start | bytes 1572868 | tf_op jit(solution)/shard_map/cond
  191.4 11.3 %copy-start.1 = (bf16[64,64,256]{2,1,0:T(8,128)(2,1)S(1)}, bf16[64,64,256]{2,1,0:T(8,128)(2,1)}, u32[]{:S(2)}) copy-start(bf16[64,64,256]{2,1,0:T(8,128)(2,1)} %branch_1_fun.2) | copy-start | bytes 6291460 | tf_op jit(solution)/shard_map/cond

commit v3 on v2

--- a/solution.py
+++ b/solution.py
@@ -28,6 +28,14 @@
     return lax.dot_general(a, b, (dims, ((), ())), precision=highest, preferred_element_type=f32)
 
 
+def dot_narrow(a, b, dims):
+    high = a.astype(jnp.bfloat16)
+    low = (a - high.astype(f32)).astype(jnp.bfloat16)
+    one = functools.partial(lax.dot_general, dimension_numbers=(dims, ((), ())),
+                            preferred_element_type=f32)
+    return one(high, b) + one(low, b)
+
+
 def conv_silu(scratch, x_ref, tail_ref, w_ref, b_ref):
     steps = x_ref.shape[0]
     scratch[0:8, :] = tail_ref[...]
@@ -41,8 +49,8 @@
 def widen(cols):
     head = lax.broadcasted_iota(jnp.int32, (HB, HBW), 0)
     lane = lax.broadcasted_iota(jnp.int32, (HB, HBW), 1)
-    spread = jnp.where(lane // HEAD_P == head, 1.0, 0.0).astype(f32)
-    return dot(cols, spread, ((1,), (0,)))
+    spread = jnp.where(lane // HEAD_P == head, 1.0, 0.0).astype(jnp.bfloat16)
+    return dot_narrow(cols, spread, ((1,), (0,)))
 
 
 def scan_kernel(
@@ -83,8 +91,8 @@
 
 def prefix_kernel(len_ref, y_ref, c_ref, cum_ref, state_ref, out_ref):
     steps = y_ref.shape[0]
-    state = state_ref[...].reshape(HBW, NSTATE).astype(f32)
-    carried = dot(c_ref[...], state, ((1,), (1,)))
+    state = state_ref[...].reshape(HBW, NSTATE)
+    carried = dot_narrow(c_ref[...], state, ((1,), (1,)))
     total = y_ref[...] + carried * widen(jnp.exp(cum_ref[0]))
     row = lax.broadcasted_iota(jnp.int32, (steps, HBW), 0)
     out_ref[...] = jnp.where(row < len_ref[0], total, 0.0).astype(jnp.bfloat16)

time: 205 us -> 203 us (level)
  Pallas kernels: 116 us -> 111 us
    pallas_call x1, Pallas kernels: 11.3 us -> 8.63 us  [prefix(): pl.pallas_call(prefix_kernel, grid=(blocks,), in_specs=[pl.BlockSpec(memo...]
    pallas_call x1, Pallas kernels: 32 us -> 29.8 us  [per_device(): pl.pallas_call(scan_kernel, grid=(groups_here, BLOCKS), in_specs=[xs(step...]
  transfers between devices with their start and end apart: 6 -> 6, of which waited for: 4 -> 4; matrix products, arithmetic and copies ran while one was open for 10% -> 10% of each run, Pallas kernels for 16% -> 15%
where the time goes in v3:
time: 203 us; the launch traced here: 201 us
  Pallas kernels  111 us (55%)
  waiting for transfers between devices  39.9 us (20%)
  starting transfers between devices  18.4 us (9%)
  local copies, waits for them, and re-layouts  15.6 us (8%)
  between operations  8.54 us (4%)
  other arithmetic  8.2 us (4%)
    pallas_call x1, Pallas kernels, relay(): pl.pallas_call(functools.partial(relay_kernel, n, chunks), in_specs=[pl.B...  62.8 us
    ppermute x3, waiting for transfers between devices, per_device(): lax.ppermute(row, 'cache', [(i, (i + shift) % n) for i in range(n)])  34.5 us
    pallas_call x1, Pallas kernels, per_device(): pl.pallas_call(scan_kernel, grid=(groups_here, BLOCKS), in_specs=[xs(step...  29.8 us
    pallas_call x1, Pallas kernels, prefix(): pl.pallas_call(prefix_kernel, grid=(blocks,), in_specs=[pl.BlockSpec(memo...  8.63 us
    all_to_all x1, starting transfers between devices, move_state(): lax.all_to_all(pieces, 'cache', split_axis=0, concat_axis=0, tiled=True)  6.46 us
    all_to_all x1, waiting for transfers between devices, move_state(): lax.all_to_all(chosen, 'cache', split_axis=0, concat_axis=0, tiled=True)  5.41 us
    pallas_call x1, Pallas kernels, per_device(): pl.pallas_call(final_kernel, grid=(blocks,), in_specs=[pl.BlockSpec(memor...  5.17 us
    ppermute x3, starting transfers between devices, per_device(): lax.ppermute(row, 'cache', [(i, (i + shift) % n) for i in range(n)])  4.92 us
  transfers between devices with their start and end apart: 6, of which 4 were waited for; matrix products, arithmetic and copies ran while one was open for 10% of the time, Pallas kernels for 15%

profile of v3, /device:TPU:0, one launch (start us, length us, event | category | flops | bytes accessed | tf_op | source)
XLA Modules:
  0.0 201.4 jit_solution(2481800131799126571)
XLA Ops:
  0.7 6.5 %all-to-all-start.2 = ((bf16[4,16,64,256]{3,2,1,0:T(8,128)(2,1)}), bf16[4,16,64,256]{3,2,1,0:T(8,128)(2,1)S(1)}, u32[]{:S(2)}, u32[]{:S(2)}) async-start(bf16[4,16,64,256]{3,2,1,0:T(8,128)(2,1)} %bitcast.68), calls=%async_computation.2 | async-start | bytes 4194304 | tf_op jit(solution)/shard_map/all_to_all | solution.py:134
  7.8 1.0 constant_dynamic-slice_fusion.4
  10.9 0.6 fusion.16
  11.5 3.8 %collective-permute-start.2 = (bf16[241,128]{1,0:T(8,128)(2,1)}, bf16[241,128]{1,0:T(8,128)(2,1)}, u32[]{:S(2)}, u32[]{:S(2)}) collective-permute-start(bf16[241,128]{1,0:T(8,128)(2,1)} %get-tuple-element.74), channel_id=1, source_target_pairs={{0,12},{4,0},{8,4},{12,8},{1,13},{5,1},{9,5},{13,9},{2,14},{6,2},{... | collective-permute-start | bytes 185096 | tf_op jit(solution)/shard_map/ppermute | solution.py:315
  15.3 1.1 collective-permute-start.1
  17.5 0.7 copy_bitcast_fusion
  18.2 1.3 copy.36
  20.4 1.3 broadcast_in_dim.64
  21.8 1.4 reshape_reshape.3.skip_ref
  23.2 0.8 fusion.3.decay_ref
  24.0 2.4 %multiply_bitcast_fusion.step_ref = f32[8,256,8]{2,1,0:T(8,128)} fusion(pred[256,8,8]{2,0,1:T(8,128)(4,1)S(1)} %copy.34, f32[256,8,8]{2,0,1:T(8,128)S(1)} %copy.35, f32[256]{0:T(256)} %copy-done.7), kind=kLoop, calls=%fused_computation | loop fusion | flops 98304 | bytes 148480 | tf_op jit(solution)/shard_map/transpose | solution.py:343
  26.4 17.3 %collective-permute-done.2 = bf16[241,128]{1,0:T(8,128)(2,1)} collective-permute-done((bf16[241,128]{1,0:T(8,128)(2,1)}, bf16[241,128]{1,0:T(8,128)(2,1)}, u32[]{:S(2)}, u32[]{:S(2)}) %collective-permute-start.2) | collective-permute-done | bytes 61728 | tf_op jit(solution)/shard_map/ppermute | solution.py:315
  43.7 4.9 %collective-permute-done = bf16[241,128]{1,0:T(8,128)(2,1)} collective-permute-done((bf16[241,128]{1,0:T(8,128)(2,1)}, bf16[241,128]{1,0:T(8,128)(2,1)}, u32[]{:S(2)}, u32[]{:S(2)}) %collective-permute-start) | collective-permute-done | bytes 61728 | tf_op jit(solution)/shard_map/ppermute | solution.py:315
  48.6 12.3 %collective-permute-done.1 = bf16[241,128]{1,0:T(8,128)(2,1)} collective-permute-done((bf16[241,128]{1,0:T(8,128)(2,1)}, bf16[241,128]{1,0:T(8,128)(2,1)}, u32[]{:S(2)}, u32[]{:S(2)}) %collective-permute-start.1) | collective-permute-done | bytes 61728 | tf_op jit(solution)/shard_map/ppermute | solution.py:315
  60.9 0.9 pad_maximum_fusion
  61.9 0.8 slice_reduce_fusion.1
  62.8 0.6 dynamic_slice.41
  65.3 1.3 copy-done
  66.6 4.3 %shard_map.149 = bf16[4,16,64,256]{3,2,1,0:T(8,128)(2,1)} custom-call(s32[4]{0:T(128)} %get-tuple-element.58.slot_ref, s32[4]{0:T(128)} %get-tuple-element.57.mask_ref, bf16[4,16,64,256]{3,2,1,0:T(8,128)(2,1)} %copy-done), custom_call_target="tpu_custom_call" | custom-call | bytes 4194304 | tf_op jit(solution)/shard_map/pallas_call | solution.py:117
  70.9 3.7 %all-to-all-start.3 = ((bf16[4,16,64,256]{3,2,1,0:T(8,128)(2,1)}), bf16[4,16,64,256]{3,2,1,0:T(8,128)(2,1)S(1)}, u32[]{:S(2)}, u32[]{:S(2)}) async-start(bf16[4,16,64,256]{3,2,1,0:T(8,128)(2,1)} %shard_map.149), calls=%async_computation.3 | async-start | bytes 4194304 | tf_op jit(solution)/shard_map/all_to_all | solution.py:136
  77.6 1.4 stack.39
  79.1 0.6 reduce_max.18
  81.6 3.3 %collective-permute-start.3 = (s32[]{:T(128)}, s32[]{:T(128)}, u32[]{:S(2)}, u32[]{:S(2)}) collective-permute-start(s32[]{:T(128)} %max.19), channel_id=1, source_target_pairs={{0,16},{16,0},{1,17},{17,1},{2,18},{18,2},{3,19},{19,3},{4,20},{20... | collective-permute-start | bytes 20 | tf_op jit(solution)/shard_map/ppermute | solution.py:439
  85.5 0.7 pad_convert_fusion.tailx_ref.tailbc_ref
  86.2 29.8 %shard_map.148 = (f32[256,4096]{1,0:T(8,128)}, f32[256,512]{1,0:T(8,128)}, f32[64,64,256]{2,1,0:T(8,128)}) custom-call(bf16[256,5120]{1,0:T(8,128)(2,1)} %bitcast.73, bf16[256,5120]{1,0:T(8,128)(2,1)} %bitcast.74, f32[8,5120]{1,0:T(8,128)} %pad_convert_fusion.tailx_ref.tailbc_ref, f32[8,5120]{1,0:T(8,128)} %pad_convert_fusion.tailx_ref.tailbc_ref, ...), custom_call_target="tpu_custom_call" | custom-call | flops 20000000000 | bytes 12000000 | tf_op jit(solution)/shard_map/pallas_call | solution.py:358
  116.6 5.4 %all-to-all-done.3 = bf16[4,16,64,256]{3,2,1,0:T(8,128)(2,1)S(1)} async-done(((bf16[4,16,64,256]{3,2,1,0:T(8,128)(2,1)}), bf16[4,16,64,256]{3,2,1,0:T(8,128)(2,1)S(1)}, u32[]{:S(2)}, u32[]{:S(2)}) %all-to-all-start.3) | async-done | bytes 2097184 | tf_op jit(solution)/shard_map/all_to_all | solution.py:136
  122.0 1.3 copy-done.2
  123.4 5.2 %shard_map.150 = bf16[64,64,256]{2,1,0:T(8,128)(2,1)S(1)} custom-call(f32[64]{0:T(128)} %fusion.3.decay_ref, f32[64,64,256]{2,1,0:T(8,128)} %get-tuple-element.52.add_ref, bf16[64,64,256]{2,1,0:T(8,128)(2,1)} %bitcast.65), custom_call_target="tpu_custom_call" | custom-call | flops 2000000 | bytes 8000000 | tf_op jit(solution)/shard_map/pallas_call | solution.py:393
  128.5 71.5 %conditional.1 = (bf16[1,64,64,256]{3,2,1,0:T(8,128)(2,1)S(1)}, bf16[1,256,4096]{2,1,0:T(8,128)(2,1)}) conditional(s32[]{:T(128)} %convert_element_type.39, (bf16[64,64,256]{2,1,0:T(8,128)(2,1)S(1)}, s32[4]{0:T(128)S(1)}, s32[1]{0:T(128)}, f32[256,4096]{1,0:T(8,128)}, f32[256,512]{1,0:T(8,128)}, /*index=5*/f32[8,256,8]{2,1,0:T(8,128)S(1)}, ...), branch_computations={%region_9.10_spmd, %region_10.11_spmd} | conditional | flops 6000000000 | bytes 127874472 | solution.py:440
  128.6 62.8 %branch_1_fun.2 = bf16[64,64,256]{2,1,0:T(8,128)(2,1)} custom-call(s32[5]{0:T(128)S(1)} %get-tuple-element.37.pick_ref, bf16[64,64,256]{2,1,0:T(8,128)(2,1)S(1)} %get-tuple-element.38.own_ref), custom_call_target="tpu_custom_call" | custom-call | bytes 100000000 | tf_op jit(solution)/shard_map/cond/branch_1_fun/pallas_call | solution.py:257
  191.4 8.6 %branch_1_fun.3 = bf16[256,4096]{1,0:T(8,128)(2,1)} custom-call(s32[1]{0:T(128)} %get-tuple-element.39.len_ref, f32[256,4096]{1,0:T(8,128)} %get-tuple-element.40.y_ref, f32[256,512]{1,0:T(8,128)S(1)} %copy-done.10, f32[8,256,8]{2,1,0:T(8,128)S(1)} %get-tuple-element.42.cum_ref, bf16[64,64,256]{2,1,0:T(8,128)(2,1)S(1)} %copy-done.3), custom_call_target="tpu_custom_call" | custom-call | flops 6000000000 | bytes 9000000 | tf_op jit(solution)/shard_map/cond/branch_1_fun/pallas_call | solution.py:408
  200.1 1.3 copy.54
  (53 shorter events, 5.2 us)
Async XLA Ops:
  0.6 10.1 %copy-start.6 = (bf16[1,3,5120]{2,1,0:T(4,128)(2,1)S(1)}, bf16[1,3,5120]{2,1,0:T(4,128)(2,1)}, u32[]{:S(2)}) copy-start(bf16[1,3,5120]{2,1,0:T(4,128)(2,1)} %param.23) | copy-start | bytes 92164
  0.6 15.8 %copy-start.8 = (f32[64]{0:T(128)S(1)}, f32[64]{0:T(128)}, u32[]{:S(2)}) copy-start(f32[64]{0:T(128)} %param.19) | copy-start | bytes 772
  0.7 15.9 %copy-start.9 = (f32[64]{0:T(128)S(1)}, f32[64]{0:T(128)}, u32[]{:S(2)}) copy-start(f32[64]{0:T(128)} %param.20) | copy-start | bytes 772
  0.7 15.9 %copy-start.5 = (f32[1,256,64]{1,2,0:T(8,128)S(1)}, f32[1,256,64]{1,2,0:T(8,128)}, u32[]{:S(2)}) copy-start(f32[1,256,64]{1,2,0:T(8,128)} %param.16) | copy-start | bytes 196612
  0.7 64.6 %all-to-all-start.2 = ((bf16[4,16,64,256]{3,2,1,0:T(8,128)(2,1)}), bf16[4,16,64,256]{3,2,1,0:T(8,128)(2,1)S(1)}, u32[]{:S(2)}, u32[]{:S(2)}) async-start(bf16[4,16,64,256]{3,2,1,0:T(8,128)(2,1)} %bitcast.68), calls=%async_computation.2 | async-start | bytes 4194304 | tf_op jit(solution)/shard_map/all_to_all | solution.py:134
  11.5 32.1 %collective-permute-start.2 = (bf16[241,128]{1,0:T(8,128)(2,1)}, bf16[241,128]{1,0:T(8,128)(2,1)}, u32[]{:S(2)}, u32[]{:S(2)}) collective-permute-start(bf16[241,128]{1,0:T(8,128)(2,1)} %get-tuple-element.74), channel_id=1, source_target_pairs={{0,12},{4,0},{8,4},{12,8},{1,13},{5,1},{9,5},{13,9},{2,14},{6,2},{... | collective-permute-start | bytes 185096 | tf_op jit(solution)/shard_map/ppermute | solution.py:315
  15.3 33.2 %collective-permute-start = (bf16[241,128]{1,0:T(8,128)(2,1)}, bf16[241,128]{1,0:T(8,128)(2,1)}, u32[]{:S(2)}, u32[]{:S(2)}) collective-permute-start(bf16[241,128]{1,0:T(8,128)(2,1)} %get-tuple-element.74), channel_id=1, source_target_pairs={{0,4},{4,8},{8,12},{12,0},{1,5},{5,9},{9,13},{13,1},{2,6},{6,10},{... | collective-permute-start | bytes 185096 | tf_op jit(solution)/shard_map/ppermute | solution.py:315
  15.3 45.5 %collective-permute-start.1 = (bf16[241,128]{1,0:T(8,128)(2,1)}, bf16[241,128]{1,0:T(8,128)(2,1)}, u32[]{:S(2)}, u32[]{:S(2)}) collective-permute-start(bf16[241,128]{1,0:T(8,128)(2,1)} %get-tuple-element.74), channel_id=1, source_target_pairs={{0,8},{4,12},{8,0},{12,4},{1,9},{5,13},{9,1},{13,5},{2,10},{6,14},... | collective-permute-start | bytes 185096 | tf_op jit(solution)/shard_map/ppermute | solution.py:315
  16.5 0.8 copy-start.7
  65.3 1.3 copy-start
  70.9 15.3 %copy-start.4 = (f32[256,8,8]{2,0,1:T(8,128)S(1)}, f32[256,8,8]{2,0,1:T(8,128)}, u32[]{:S(2)}) copy-start(f32[256,8,8]{2,0,1:T(8,128)} %copy.36) | copy-start | bytes 196612
  70.9 51.1 %all-to-all-start.3 = ((bf16[4,16,64,256]{3,2,1,0:T(8,128)(2,1)}), bf16[4,16,64,256]{3,2,1,0:T(8,128)(2,1)S(1)}, u32[]{:S(2)}, u32[]{:S(2)}) async-start(bf16[4,16,64,256]{3,2,1,0:T(8,128)(2,1)} %shard_map.149), calls=%async_computation.3 | async-start | bytes 4194304 | tf_op jit(solution)/shard_map/all_to_all | solution.py:136
  81.6 34.4 %collective-permute-start.3 = (s32[]{:T(128)}, s32[]{:T(128)}, u32[]{:S(2)}, u32[]{:S(2)}) collective-permute-start(s32[]{:T(128)} %max.19), channel_id=1, source_target_pairs={{0,16},{16,0},{1,17},{17,1},{2,18},{18,2},{3,19},{19,3},{4,20},{20... | collective-permute-start | bytes 20 | tf_op jit(solution)/shard_map/ppermute | solution.py:439
  122.0 1.3 copy-start.2
  128.6 62.8 %copy-start.3 = (bf16[64,64,256]{2,1,0:T(8,128)(2,1)S(1)}, bf16[64,64,256]{2,1,0:T(8,128)(2,1)}, u32[]{:S(2)}) copy-start(bf16[64,64,256]{2,1,0:T(8,128)(2,1)} %get-tuple-element.43.state_ref) | copy-start | bytes 6291460 | tf_op jit(solution)/shard_map/cond
  128.6 62.8 %copy-start.10 = (f32[256,512]{1,0:T(8,128)S(1)}, f32[256,512]{1,0:T(8,128)}, u32[]{:S(2)}) copy-start(f32[256,512]{1,0:T(8,128)} %get-tuple-element.41.c_ref) | copy-start | bytes 1572868 | tf_op jit(solution)/shard_map/cond
  191.4 8.6 %copy-start.1 = (bf16[64,64,256]{2,1,0:T(8,128)(2,1)S(1)}, bf16[64,64,256]{2,1,0:T(8,128)(2,1)}, u32[]{:S(2)}) copy-start(bf16[64,64,256]{2,1,0:T(8,128)(2,1)} %branch_1_fun.2) | copy-start | bytes 6291460 | tf_op jit(solution)/shard_map/cond
